TPU v7x, 32 devices: a whole 2x2x4 slice. The times are simulated.
32 devices in a mesh: sens: 1, samp: 32 (over z, y, x, core).
Axes of the slice: x: 2, y: 2, z: 4, core: 2. Of those that a mesh axis runs over, the one named last changes fastest.
Arguments:
- slopes: bfloat16 [2, 128, 37632], P(None, 'samp', 'sens'), may hold values from -0.0625 to 0.0625
- targets: bfloat16 [2, 8192, 128], P(None, 'samp'), may hold values from -6 to 6
- reconstructor: float32 [1, 32, 32, 128, 128], P('sens', 'samp'), may hold values from -6 to 6
- foot_act: int32 [1, 32, 32], P('sens'), may hold values from 0 to 1, as said below
- foot_slope: int32 [1, 32, 32], P('sens'), may hold values from 0 to 293, as said below
- foot_count: int32 [1, 32], P('sens'), may hold values from 16 to 32, as said below
Outputs:
- fitted: float32 [1, 32, 32, 128, 128], P('sens', 'samp')
- fit_residual: bfloat16 [8192, 128], P('samp')
Inputs may be any that keep to these rules, and one draw needn't show every extreme that they name: `foot_act`: slots 0 to foot_count-1 of a device are live, the rest padding (actuator block 0 and a slope block already named by slot 0); no (actuator block, slope block) pair repeats among live slots; the slope blocks of one actuator block form a run of consecutive blocks modulo 294. `foot_slope`: the live slots of one device name at most 20 distinct slope blocks; for every sens index some device names exactly 20. `foot_count`: for every sens index some device has 32 live slots.
All inputs are finite; a program needn't handle non-finite values.
Results may differ from a plain program's by a relative error of at most 0.0037.
Values may be sent and summed in bfloat16 or wider, within the bound.
No kernel may reach another device: no remote copies, remote signals or barrier semaphores. Data moves between devices by JAX's collectives and lax.ppermute only.
A program may use at most 64 MiB of HBM per device.

v0:
```python
import jax
import jax.numpy as jnp
from jax import lax
from jax.sharding import PartitionSpec as P

STEPS = 2


def per_device(slopes, targets, reconstructor, foot_act, foot_slope, foot_count):
    samp_count = lax.axis_size("samp")
    own_index = lax.axis_index("samp")
    block_size = reconstructor.shape[-1]
    slot_count = reconstructor.shape[2]
    groups = slopes.shape[2] // block_size
    samp_dev = slopes.shape[1]
    act_blocks = targets.shape[1] // block_size
    samples = targets.shape[2]
    step_rate = slot_count * block_size / (samples + 3 * slot_count * block_size)
    act_all = foot_act[0]
    slope_all = foot_slope[0]
    count_all = foot_count[0]
    live_all = jnp.arange(slot_count)[None, :] < count_all[:, None]
    own_act = lax.dynamic_index_in_dim(act_all, own_index, 0, keepdims=False)
    own_live = lax.dynamic_index_in_dim(live_all, own_index, 0, keepdims=False)
    act_onehot = ((own_act[None, :] == jnp.arange(act_blocks)[:, None]) & own_live[None, :]).astype(
        jnp.float32
    )
    need_count = slope_all.shape[1]
    weights = reconstructor[0, 0]
    fit_residual = None
    for step in range(STEPS):
        local_rows = slopes[step].reshape(samp_dev, groups, block_size)
        outgoing = jnp.take(local_rows, slope_all.reshape(-1), axis=1)
        outgoing = outgoing.reshape(samp_dev, samp_count, need_count, block_size)
        arrived = lax.all_to_all(outgoing, "samp", split_axis=1, concat_axis=0, tiled=True)
        slot_slopes = arrived.reshape(samples, need_count, block_size)
        weights_low = weights.astype(jnp.bfloat16)
        partial_sums = jnp.einsum(
            "kil,nkl->kin", weights_low, slot_slopes, preferred_element_type=jnp.float32
        )
        summed = jnp.einsum(
            "jk,kin->jin", act_onehot, partial_sums, precision=lax.Precision.HIGHEST
        )
        target_now = targets[step].reshape(act_blocks, block_size, samples)
        total = lax.psum(summed, "sens")
        residual = (total - target_now).astype(jnp.bfloat16)
        slot_residual = jnp.take(residual, own_act, axis=0)
        gradient = jnp.einsum(
            "kin,nkl->kil", slot_residual, slot_slopes, preferred_element_type=jnp.float32
        )
        weights = jnp.where(own_live[:, None, None], weights - step_rate * gradient, weights)
        fit_residual = residual
    return (weights[None, None], fit_residual.reshape(act_blocks * block_size, samples))


def solution(mesh):
    return jax.shard_map(
        per_device,
        mesh=mesh,
        in_specs=(
            P(None, "samp", "sens"),
            P(None, "samp", None),
            P("sens", "samp", None, None, None),
            P("sens", None, None),
            P("sens", None, None),
            P("sens", None),
        ),
        out_specs=(P("sens", "samp", None, None, None), P("samp", None)),
        check_vma=False,
    )
```

profile of v0, /device:TPU:0, one launch (start us, length us, event | category | flops | bytes accessed | tf_op | source)
XLA Modules:
  0.0 93.0 jit_solution(4637839867910024543)
XLA Ops:
  0.6 0.8 reshape_squeeze.13
  1.4 1.3 %slice_bitcast_fusion = (bf16[4,294,128]{2,0,1:T(4,128)(2,1)S(1)}, bf16[4,294,128]{2,0,1:T(4,128)(2,1)S(1)}) fusion(bf16[2,4,37632]{2,1,0:T(4,128)(2,1)} %param.10), kind=kLoop, calls=%fused_computation.21 | loop fusion | bytes 1204224 | tf_op jit(solution)/shard_map/reshape;squeeze | solution.py:32
  2.7 3.6 %gather_fusion = bf16[1024,4,128]{2,1,0:T(4,128)(2,1)S(1)} fusion(bf16[4,294,128]{2,0,1:T(4,128)(2,1)S(1)} %get-tuple-element.7, s32[1024]{0:T(1024)S(1)} %fusion.13), kind=kCustom, calls=%fused_computation.clone | custom fusion | bytes 2101248 | tf_op jit(solution)/shard_map/jit(_take)/gather | solution.py:33
  6.3 3.6 %gather_fusion.2 = bf16[1024,4,128]{2,1,0:T(4,128)(2,1)S(1)} fusion(bf16[4,294,128]{2,0,1:T(4,128)(2,1)S(1)} %get-tuple-element.6, s32[1024]{0:T(1024)S(1)} %fusion.13), kind=kCustom, calls=%fused_computation.2.clone | custom fusion | bytes 2101248 | tf_op jit(solution)/shard_map/jit(_take)/gather | solution.py:33
  9.9 3.8 %broadcast_select_fusion = (bf16[1024,4,128]{2,1,0:T(4,128)(2,1)S(1)}, bf16[1024,4,128]{2,1,0:T(4,128)(2,1)S(1)}) fusion(bf16[1024,4,128]{2,1,0:T(4,128)(2,1)S(1)} %gather_fusion.2, pred[1024]{0:T(1024)(128)(4,1)S(1)} %compare_and_fusion, bf16[1024,4,128]{2,1,0:T(4,128)(2,1)S(1)} %gather_fusion), kind=kLoop, calls=%fused_computation.15 | loop fusion | flops 1048576 | bytes 4195328 | tf_op jit(solution)/shard_map/jit(_take)/select_n | solution.py:33
  13.7 1.2 %copy.49 = bf16[4,32,32,128]{3,2,0,1:T(8,128)(2,1)} copy(bf16[4,32,32,128]{3,0,2,1:T(4,128)(2,1)S(1)} %bitcast.62) | data formatting | bytes 2097152 | tf_op jit(solution)/shard_map/reshape | solution.py:34
  14.9 7.3 %all-to-all-start = ((bf16[4,32,32,128]{3,2,0,1:T(8,128)(2,1)}), bf16[4,32,32,128]{3,2,0,1:T(8,128)(2,1)S(1)}, u32[]{:S(2)}, u32[]{:S(2)}) async-start(bf16[4,32,32,128]{3,2,0,1:T(8,128)(2,1)} %copy.49), calls=%async_computation | async-start | bytes 2097152 | tf_op jit(solution)/shard_map/all_to_all | solution.py:35
  22.2 0.0 copy-start.4
  22.2 0.0 copy-start.3
  22.2 1.2 %copy.55 = bf16[4,32,32,128]{3,2,0,1:T(8,128)(2,1)} copy(bf16[4,32,32,128]{3,0,2,1:T(4,128)(2,1)S(1)} %bitcast.61) | data formatting | bytes 2097152 | tf_op jit(solution)/shard_map/reshape | solution.py:34
  23.4 0.0 copy-start.2
  23.4 25.0 %all-to-all-done = bf16[4,32,32,128]{3,2,0,1:T(8,128)(2,1)S(1)} async-done(((bf16[4,32,32,128]{3,2,0,1:T(8,128)(2,1)}), bf16[4,32,32,128]{3,2,0,1:T(8,128)(2,1)S(1)}, u32[]{:S(2)}, u32[]{:S(2)}) %all-to-all-start) | async-done | bytes 1048608 | tf_op jit(solution)/shard_map/all_to_all | solution.py:35
  48.4 3.7 %all-to-all-start.1 = ((bf16[4,32,32,128]{3,2,0,1:T(8,128)(2,1)}), bf16[4,32,32,128]{3,2,0,1:T(8,128)(2,1)}, u32[]{:S(2)}, u32[]{:S(2)}) async-start(bf16[4,32,32,128]{3,2,0,1:T(8,128)(2,1)} %copy.55), calls=%async_computation.1 | async-start | bytes 2097152 | tf_op jit(solution)/shard_map/all_to_all | solution.py:35
  52.2 0.0 copy-done.4
  52.2 0.6 dynamic-slice.1
  52.8 0.7 compare_bitcast_fusion
  53.4 0.7 compare_and_fusion.1
  54.2 0.0 copy-done.3
  54.2 0.5 copy.50
  54.7 0.0 copy-start.1
  54.8 1.0 %copy-done.1 = bf16[32,4,1,32,128]{4,1,0,3,2:T(4,128)(2,1)} copy-done((bf16[32,4,1,32,128]{4,1,0,3,2:T(4,128)(2,1)}, bf16[32,4,1,32,128]{4,1,0,3,2:T(4,128)(2,1)S(1)}, u32[]{:S(2)}) %copy-start.1) | copy-done | bytes 1048600
  55.8 0.0 copy-done.2
  55.8 2.2 %convolution_bitcast_fusion = f32[32,128,128]{1,2,0:T(8,128)} fusion(bf16[128,32,128]{2,0,1:T(8,128)(2,1)S(1)} %bitcast.59, f32[1,1,32,128,128]{4,3,2,1,0:T(8,128)S(1)} %copy-done.2), kind=kOutput, calls=%fused_computation.10 | convolution fusion | flops 134217728 | bytes 5242880 | tf_op jit(solution)/shard_map/kil,nkl->kin/dot_general | solution.py:38
  57.9 2.4 %copy.51 = f32[32,128,128]{2,0,1:T(8,128)S(1)} copy(f32[32,128,128]{1,2,0:T(8,128)} %convolution_bitcast_fusion) | data formatting | bytes 4194304 | tf_op jit(solution)/shard_map/kil,nkl->kin/dot_general | solution.py:38
  60.3 18.1 %all-to-all-done.1 = bf16[4,32,32,128]{3,2,0,1:T(8,128)(2,1)} async-done(((bf16[4,32,32,128]{3,2,0,1:T(8,128)(2,1)}), bf16[4,32,32,128]{3,2,0,1:T(8,128)(2,1)}, u32[]{:S(2)}, u32[]{:S(2)}) %all-to-all-start.1) | async-done | bytes 1048608 | tf_op jit(solution)/shard_map/all_to_all | solution.py:35
  78.4 1.8 %copy.56 = bf16[32,4,1,32,128]{4,1,0,3,2:T(4,128)(2,1)S(1)} copy(bf16[32,4,1,32,128]{4,3,1,0,2:T(8,128)(2,1)} %bitcast.17) | data formatting | bytes 2097152 | tf_op jit(solution)/shard_map/all_to_all | solution.py:35
  80.2 0.8 fusion.15
  81.0 1.7 %gather_fusion.1 = bf16[32,128,128]{2,1,0:T(8,128)(2,1)} fusion(bf16[2,128,128]{2,1,0:T(8,128)(2,1)S(1)} %fusion.12, s32[1024]{0:T(1024)S(1)} %pad_clamp_fusion), kind=kCustom, calls=%fused_computation.1.clone | custom fusion | bytes 2097280 | tf_op jit(solution)/shard_map/jit(_take)/gather | solution.py:47
  82.7 2.7 %subtract_select_fusion.1 = f32[32,128,128]{2,1,0:T(8,128)S(1)} fusion(f32[1,1,32,128,128]{4,3,2,1,0:T(8,128)} %param.12, bf16[128,32,128]{2,0,1:T(8,128)(2,1)} %bitcast.60, bf16[32,128,128]{2,1,0:T(8,128)(2,1)} %gather_fusion.1, pred[32]{0:T(512)(128)(4,1)S(1)} %get-tuple-element.4, pred[32]{0:T(512)(128)(4,1)S(1)} %compare_bitcast_fusion), kind=kOutput, calls=%fused_computation.5 | convolution fusion | flops 136314880 | bytes 6291520 | tf_op jit(solution)/shard_map/kin,nkl->kil/dot_general | solution.py:48
  85.4 0.8 fusion.5
  86.3 2.0 %fusion.1 = f32[2,128,128]{2,0,1:T(2,128)S(1)} fusion(f32[32,128,128]{2,1,0:T(8,128)S(1)} %fusion.5, pred[32]{0:T(512)(128)(4,1)S(1)} %compare_bitcast_fusion, s32[32]{0:T(128)S(1)} %get-tuple-element.5), kind=kOutput, calls=%fused_computation.8 | convolution fusion | flops 12583040 | bytes 2228384 | tf_op jit(solution)/shard_map/jk,kin->jin/dot_general | solution.py:41
  88.3 0.0 copy-start
  88.3 1.7 %gather_fusion.3 = bf16[32,128,128]{2,1,0:T(8,128)(2,1)} fusion(bf16[2,128,128]{2,1,0:T(8,128)(2,1)S(1)} %fusion.11, s32[1024]{0:T(1024)S(1)} %pad_clamp_fusion), kind=kCustom, calls=%fused_computation.3.clone | custom fusion | bytes 2097280 | tf_op jit(solution)/shard_map/jit(_take)/gather | solution.py:47
  89.9 3.1 %fusion = f32[1,1,32,128,128]{4,3,2,1,0:T(8,128)} fusion(f32[32,128,128]{2,1,0:T(8,128)S(1)} %subtract_select_fusion.1, bf16[128,32,128]{2,0,1:T(8,128)(2,1)S(1)} %bitcast.58, bf16[32,128,128]{2,1,0:T(8,128)(2,1)} %gather_fusion.3, pred[32]{0:T(512)(128)(4,1)S(1)} %get-tuple-element.4, pred[32]{0:T(512)(128)(4,1)S(1)} %compare_bitcast_fusion), kind=kOutput, calls=%fused_computation.6 | convolution fusion | flops 136314880 | bytes 6291520 | tf_op jit(solution)/shard_map/kin,nkl->kil/dot_general | solution.py:48
  93.0 0.0 copy-done
  (7 shorter events, 0.1 us)
Async XLA Ops:
  14.9 33.5 %all-to-all-start = ((bf16[4,32,32,128]{3,2,0,1:T(8,128)(2,1)}), bf16[4,32,32,128]{3,2,0,1:T(8,128)(2,1)S(1)}, u32[]{:S(2)}, u32[]{:S(2)}) async-start(bf16[4,32,32,128]{3,2,0,1:T(8,128)(2,1)} %copy.49), calls=%async_computation | async-start | bytes 2097152 | tf_op jit(solution)/shard_map/all_to_all | solution.py:35
  22.2 30.0 %copy-start.4 = (s32[1,32]{1,0:T(1,128)S(1)}, s32[1,32]{1,0:T(1,128)}, u32[]{:S(2)}) copy-start(s32[1,32]{1,0:T(1,128)} %param.15) | copy-start | bytes 388
  22.2 32.0 %copy-start.3 = (bf16[2,256,128]{2,1,0:T(8,128)(2,1)S(1)}, bf16[2,256,128]{2,1,0:T(8,128)(2,1)}, u32[]{:S(2)}) copy-start(bf16[2,256,128]{2,1,0:T(8,128)(2,1)} %param.11) | copy-start | bytes 393220
  23.4 32.3 %copy-start.2 = (f32[1,1,32,128,128]{4,3,2,1,0:T(8,128)S(1)}, f32[1,1,32,128,128]{4,3,2,1,0:T(8,128)}, u32[]{:S(2)}) copy-start(f32[1,1,32,128,128]{4,3,2,1,0:T(8,128)} %param.12) | copy-start | bytes 6291460
  48.4 30.0 %all-to-all-start.1 = ((bf16[4,32,32,128]{3,2,0,1:T(8,128)(2,1)}), bf16[4,32,32,128]{3,2,0,1:T(8,128)(2,1)}, u32[]{:S(2)}, u32[]{:S(2)}) async-start(bf16[4,32,32,128]{3,2,0,1:T(8,128)(2,1)} %copy.55), calls=%async_computation.1 | async-start | bytes 2097152 | tf_op jit(solution)/shard_map/all_to_all | solution.py:35
  54.7 1.0 %copy-start.1 = (bf16[32,4,1,32,128]{4,1,0,3,2:T(4,128)(2,1)}, bf16[32,4,1,32,128]{4,1,0,3,2:T(4,128)(2,1)S(1)}, u32[]{:S(2)}) copy-start(bf16[32,4,1,32,128]{4,1,0,3,2:T(4,128)(2,1)S(1)} %copy.50) | copy-start | bytes 3145732
  88.3 4.7 %copy-start = (bf16[2,128,128]{2,1,0:T(8,128)(2,1)}, bf16[2,128,128]{2,1,0:T(8,128)(2,1)S(1)}, u32[]{:S(2)}) copy-start(bf16[2,128,128]{2,1,0:T(8,128)(2,1)S(1)} %fusion.11) | copy-start | bytes 196612
where the time goes:
time: 93.5 us; the launch traced here: 93 us
  waiting for transfers between devices  43.1 us (46%)
  local copies, waits for them, and re-layouts  21.2 us (23%)
  matrix products  11.6 us (12%)
  starting transfers between devices  11 us (12%)
  other arithmetic  5.24 us (6%)
    all_to_all x2, waiting for transfers between devices, per_device(): lax.all_to_all(outgoing, 'samp', split_axis=1, concat_axis=0, tiled=True)  43.1 us
    all_to_all x2, starting transfers between devices, per_device(): lax.all_to_all(outgoing, 'samp', split_axis=1, concat_axis=0, tiled=True)  11 us
    gather x2, local copies, waits for them, and re-layouts, per_device(): outgoing = jnp.take(local_rows, slope_all.reshape(-1), axis=1)  7.15 us
    dot_general x2, matrix products, per_device(): jnp.einsum('kin,nkl->kil', slot_residual, slot_slopes, preferred_element_...  5.79 us
    select_n x1, other arithmetic, per_device(): outgoing = jnp.take(local_rows, slope_all.reshape(-1), axis=1)  3.82 us
    gather x2, local copies, waits for them, and re-layouts, per_device(): slot_residual = jnp.take(residual, own_act, axis=0)  3.31 us
    dot_general x2, matrix products, per_device(): jnp.einsum('kil,nkl->kin', weights_low, slot_slopes, preferred_element_ty...  3.02 us
    dot_general x2, matrix products, per_device(): jnp.einsum('jk,kin->jin', act_onehot, partial_sums, precision=lax.Precisi...  2.79 us
  transfers between devices with their start and end apart: 2, of which 2 were waited for; matrix products, arithmetic and copies ran while one was open for 9% of the time, Pallas kernels for 0%

commit v1 on v0

v1 whole, which is shorter than its diff:
```python
import functools

import jax
import jax.numpy as jnp
from jax import lax
from jax.experimental import pallas as pl
from jax.experimental.pallas import tpu as pltpu
from jax.sharding import PartitionSpec as P

STEPS = 2
DISTINCT = 20
MIB = 1 << 20


def window_starts(slope_all, count_all, groups):
    slots = slope_all.shape[1]
    half = groups // 2
    live = jnp.arange(slots)[None, :] < count_all[:, None]
    turned = jnp.where(slope_all >= groups - half, slope_all - (groups - half), slope_all + half)

    def span(blocks):
        low = jnp.min(jnp.where(live, blocks, groups), axis=1)
        high = jnp.max(jnp.where(live, blocks, -1), axis=1)
        return low, high - low < DISTINCT

    low, fits = span(slope_all)
    low_turned, fits_turned = span(turned)
    unturned = jnp.where(low_turned >= half, low_turned - half, low_turned + groups - half)
    return jnp.where(fits, low, jnp.where(fits_turned, unturned, -1)).astype(jnp.int32)


def own_places(slopes_own, count_own, start, groups):
    slots = slopes_own.shape[0]
    ids = jnp.arange(slots)
    live = ids < count_own
    same = (slopes_own[:, None] == slopes_own[None, :]) & live[None, :]
    repeated = jnp.any(same & (ids[None, :] < ids[:, None]), axis=1)
    first = live & ~repeated
    rank = jnp.sum(first[None, :] & (ids[None, :] < ids[:, None]), axis=1)
    ranked = jnp.sum(jnp.where(same & first[None, :], rank[None, :], 0), axis=1)
    offset = slopes_own - start
    offset = jnp.where(offset < 0, offset + groups, offset)
    return jnp.where(live, jnp.where(start >= 0, offset, ranked), -1).astype(jnp.int32)


def pack_kernel(starts, slope_tab, counts, slopes, out, rows, sems):
    steps, samp_dev, width = slopes.shape
    block = 128
    groups = width // block
    devices, _, window = out.shape
    span = window // block

    def join(first, last):
        cols = slice(first * block, last * block)
        return jnp.concatenate([slopes[t, :, cols] for t in range(steps)], axis=0)

    piece = 14
    for first in range(0, groups, piece):
        last = min(first + piece, groups)
        rows[:, first * block : last * block] = join(first, last)
    rows[:, width:] = join(0, span)

    def window_of(d):
        return pltpu.make_async_copy(
            rows.at[:, pl.ds(pl.multiple_of(starts[d] * block, block), window)], out.at[d], sems.at[d]
        )

    def block_to(d, group, at):
        return pltpu.make_async_copy(
            rows.at[:, pl.ds(pl.multiple_of(group * block, block), block)],
            out.at[d, :, pl.ds(pl.multiple_of(at * block, block), block)],
            sems.at[d],
        )

    def one_by_one(d):
        def slot(k, placed):
            group = slope_tab[d, k]
            seen = lax.fori_loop(
                0, k, lambda j, s: jnp.where(slope_tab[d, j] == group, 1, s), jnp.int32(0)
            )

            @pl.when(seen == 0)
            def _():
                block_to(d, group, placed).start()

            return placed + 1 - seen

        placed = lax.fori_loop(0, counts[d], slot, jnp.int32(0))

        def fill(j, carry):
            block_to(d, slope_tab[d, 0], j).start()
            return carry

        lax.fori_loop(placed, span, fill, 0)

    def send(d, carry):
        @pl.when(starts[d] >= 0)
        def _():
            window_of(d).start()

        @pl.when(starts[d] < 0)
        def _():
            one_by_one(d)

        return carry

    lax.fori_loop(0, devices, send, 0)

    def settle(d, carry):
        pltpu.make_async_copy(rows.at[:, pl.ds(0, window)], out.at[d], sems.at[d]).wait()
        return carry

    lax.fori_loop(0, devices, settle, 0)


def pack(starts, slope_all, count_all, slopes):
    steps, samp_dev, width = slopes.shape
    devices = slope_all.shape[0]
    block = 128
    tall = steps * samp_dev
    window = DISTINCT * block
    smem = pl.BlockSpec(memory_space=pltpu.SMEM)
    return pl.pallas_call(
        pack_kernel,
        out_shape=jax.ShapeDtypeStruct((devices, tall, window), slopes.dtype),
        in_specs=[smem, smem, smem, pl.BlockSpec(memory_space=pltpu.VMEM)],
        out_specs=pl.BlockSpec(memory_space=pl.ANY),
        scratch_shapes=[
            pltpu.VMEM((tall, width + window), slopes.dtype),
            pltpu.SemaphoreType.DMA((devices,)),
        ],
        compiler_params=pltpu.CompilerParams(vmem_limit_bytes=16 * MIB),
        name="pack_windows",
    )(starts, slope_all, count_all, slopes)


def stage_kernel(rate, samp_dev, places, acts, weights, targets, stack, low, spread, rates):
    steps, rows, samples = targets.shape
    slots, block, _ = weights.shape
    stack[...] = jnp.zeros_like(stack)
    low[...] = jnp.zeros_like(low)
    rates[...] = jnp.zeros_like(rates)

    def slot(k, carry):
        @pl.when(places[k] >= 0)
        def _():
            at_rows = pl.ds(pl.multiple_of(acts[k] * block, block), block)
            at_cols = pl.ds(pl.multiple_of(places[k] * block, block), block)
            now = weights[k]
            stack[at_rows, at_cols] = now
            low[at_rows, at_cols] = now.astype(low.dtype)
            rates[acts[k], :, at_cols] = jnp.full((8, block), rate, rates.dtype)

        return carry

    lax.fori_loop(0, slots, slot, 0)
    wide = spread.shape[2]
    for t in range(steps):
        spread[t] = jnp.dot(
            targets[t], spreader(samples, wide, samp_dev, t, targets.dtype), preferred_element_type=jnp.float32
        )


def spreader(samples, wide, samp_dev, step, dtype):
    tall = wide * samp_dev // samples
    n = lax.broadcasted_iota(jnp.int32, (samples, wide), 0)
    c = lax.broadcasted_iota(jnp.int32, (samples, wide), 1)
    column = (n // samp_dev) * tall + step * samp_dev + n % samp_dev
    return (c == column).astype(jnp.float32).astype(dtype)


def stage(rate, samp_dev, places, acts, weights, targets):
    steps, rows, samples = targets.shape
    block = weights.shape[-1]
    window = DISTINCT * block
    smem = pl.BlockSpec(memory_space=pltpu.SMEM)
    vmem = pl.BlockSpec(memory_space=pltpu.VMEM)
    return pl.pallas_call(
        functools.partial(stage_kernel, rate, samp_dev),
        out_shape=[
            jax.ShapeDtypeStruct((rows, window), jnp.float32),
            jax.ShapeDtypeStruct((rows, window), jnp.bfloat16),
            jax.ShapeDtypeStruct((steps, rows, steps * samples), jnp.float32),
            jax.ShapeDtypeStruct((rows // block, 8, window), jnp.float32),
        ],
        in_specs=[smem, smem, vmem, vmem],
        out_specs=[vmem, vmem, vmem, vmem],
        compiler_params=pltpu.CompilerParams(vmem_limit_bytes=16 * MIB),
        cost_estimate=pl.CostEstimate(flops=10**8, bytes_accessed=9 * 10**6, transcendentals=0),
        name="stage_weights",
    )(places, acts, weights, targets)


def fit_kernel(
    samp_dev, places, acts, seen, stack_in, low_in, spread, rates, weights, fitted, residual, stack, low, slot_of, sems
):
    steps, rows, wide = spread.shape
    slots, block, _ = weights.shape
    window = seen.shape[1]
    span = window // block
    blocks = rows // block
    samples = residual.shape[1]
    tall = wide * samp_dev // samples

    def clear(j, carry):
        slot_of[j] = -1
        return carry

    lax.fori_loop(0, blocks * span, clear, 0)

    def note(k, carry):
        @pl.when(places[k] >= 0)
        def _():
            slot_of[acts[k] * span + places[k]] = k

        @pl.when(places[k] < 0)
        def _():
            pltpu.make_async_copy(weights.at[k], fitted.at[k], sems.at[k]).start()

        return carry

    lax.fori_loop(0, slots, note, 0)

    column = lax.broadcasted_iota(jnp.int32, (rows, wide), 1)
    step_of = (column % tall) // samp_dev
    chunk = 4 * block
    for t in range(steps):
        source = low_in if t == 0 else low
        held = stack_in if t == 0 else stack
        predicted = lax.dot_general(
            source[...], seen[...], (((1,), (1,)), ((), ())), preferred_element_type=jnp.float32
        )
        rest = jnp.where(step_of == t, predicted - spread[t], 0.0).astype(jnp.bfloat16)
        if t == steps - 1:
            pick = spreader(samples, wide, samp_dev, t, jnp.bfloat16)
            residual[...] = lax.dot_general(
                rest, pick, (((1,), (1,)), ((), ())), preferred_element_type=jnp.float32
            ).astype(residual.dtype)
        for first in range(0, window, chunk):
            cols = slice(first, min(first + chunk, window))
            gradient = jnp.dot(rest, seen[:, cols], preferred_element_type=jnp.float32)
            for a in range(blocks):
                at = slice(a * block, (a + 1) * block)
                new = held[at, cols] - rates[a, 0:1, cols] * gradient[at]
                stack[at, cols] = new
                if t < steps - 1:
                    low[at, cols] = new.astype(low.dtype)
            if t == steps - 1:
                for a in range(blocks):
                    for p in range(first // block, cols.stop // block):
                        k = slot_of[a * span + p]

                        @pl.when(k >= 0)
                        def _(a=a, p=p, k=k):
                            pltpu.make_async_copy(
                                stack.at[pl.ds(a * block, block), pl.ds(p * block, block)], fitted.at[k], sems.at[k]
                            ).start()

    def settle(k, carry):
        pltpu.make_async_copy(stack.at[pl.ds(0, block), pl.ds(0, block)], fitted.at[k], sems.at[k]).wait()
        return carry

    lax.fori_loop(0, slots, settle, 0)


def fit(samp_dev, places, acts, seen, stack, low, spread, rates, weights, samples):
    rows, window = stack.shape
    slots, block, _ = weights.shape
    smem = pl.BlockSpec(memory_space=pltpu.SMEM)
    vmem = pl.BlockSpec(memory_space=pltpu.VMEM)
    anywhere = pl.BlockSpec(memory_space=pl.ANY)
    return pl.pallas_call(
        functools.partial(fit_kernel, samp_dev),
        out_shape=[
            jax.ShapeDtypeStruct(weights.shape, jnp.float32),
            jax.ShapeDtypeStruct((rows, samples), jnp.bfloat16),
        ],
        in_specs=[smem, smem, vmem, vmem, vmem, vmem, vmem, anywhere],
        out_specs=[anywhere, vmem],
        scratch_shapes=[
            pltpu.VMEM((rows, window), jnp.float32),
            pltpu.VMEM((rows, window), jnp.bfloat16),
            pltpu.SMEM((rows // block * DISTINCT,), jnp.int32),
            pltpu.SemaphoreType.DMA((slots,)),
        ],
        compiler_params=pltpu.CompilerParams(vmem_limit_bytes=32 * MIB),
        name="fit_steps",
    )(places, acts, seen, stack, low, spread, rates, weights)


def fit_over_groups(step_rate, samp_dev, places, acts, arrived, weights, targets):
    steps, rows, samples = targets.shape
    slots, block, _ = weights.shape
    live = places >= 0
    devices = arrived.shape[0]
    grouped = arrived.reshape(devices, steps, samp_dev, DISTINCT, block)
    slot_slopes = jnp.take(grouped, jnp.maximum(places, 0), axis=3)
    blocks = rows // block
    onehot = ((acts[None, :] == jnp.arange(blocks)[:, None]) & live[None, :]).astype(jnp.float32)
    residual = None
    for t in range(steps):
        now = slot_slopes[:, t].reshape(samples, slots, block)
        partial_sums = jnp.einsum(
            "kil,nkl->kin", weights.astype(jnp.bfloat16), now, preferred_element_type=jnp.float32
        )
        summed = jnp.einsum("jk,kin->jin", onehot, partial_sums, precision=lax.Precision.HIGHEST)
        total = lax.psum(summed, "sens")
        residual = (total - targets[t].reshape(blocks, block, samples)).astype(jnp.bfloat16)
        gradient = jnp.einsum(
            "kin,nkl->kil", jnp.take(residual, acts, axis=0), now, preferred_element_type=jnp.float32
        )
        weights = jnp.where(live[:, None, None], weights - step_rate * gradient, weights)
    return weights, residual.reshape(rows, samples)


def per_device(slopes, targets, reconstructor, foot_act, foot_slope, foot_count):
    own_index = lax.axis_index("samp")
    block = reconstructor.shape[-1]
    slots = reconstructor.shape[2]
    groups = slopes.shape[2] // block
    samp_dev = slopes.shape[1]
    samples = targets.shape[2]
    devices = foot_slope.shape[1]
    step_rate = slots * block / (samples + 3 * slots * block)
    starts = window_starts(foot_slope[0], foot_count[0], groups)
    packed = pack(starts, foot_slope[0], foot_count[0], slopes)
    arrived = lax.all_to_all(packed, "samp", split_axis=0, concat_axis=0, tiled=True)

    def own(table):
        return lax.dynamic_index_in_dim(table, own_index, 0, keepdims=False)

    places = own_places(own(foot_slope[0]), own(foot_count[0]), own(starts), groups)
    acts = own(foot_act[0])
    weights = reconstructor[0, 0]
    if lax.axis_size("sens") > 1:
        fitted, residual = fit_over_groups(step_rate, samp_dev, places, acts, arrived, weights, targets)
        return fitted[None, None], residual
    stack, low, spread, rates = stage(step_rate, samp_dev, places, acts, weights, targets)
    seen = arrived.reshape(devices * STEPS * samp_dev, DISTINCT * block)
    fitted, residual = fit(samp_dev, places, acts, seen, stack, low, spread, rates, weights, samples)
    return fitted[None, None], residual


def solution(mesh):
    return jax.shard_map(
        per_device,
        mesh=mesh,
        in_specs=(
            P(None, "samp", "sens"),
            P(None, "samp", None),
            P("sens", "samp", None, None, None),
            P("sens", None, None),
            P("sens", None, None),
            P("sens", None),
        ),
        out_specs=(P("sens", "samp", None, None, None), P("samp", None)),
        check_vma=False,
    )
```

time: 93.5 us -> 60 us (0.64)
  waiting for transfers between devices: 43.1 us -> 20.8 us
  matrix products: 11.6 us -> 0 us
  Pallas kernels: 0 us -> 11.6 us
  local copies, waits for them, and re-layouts: 21.2 us -> 14.5 us
  starting transfers between devices: 11 us -> 7.3 us
  other arithmetic: 5.24 us -> 3.97 us
    all_to_all x2 -> x1, waiting for transfers between devices: 43.1 us -> 20.8 us  [per_device(): lax.all_to_all(packed, 'samp', split_axis=0, concat_axis=0, tiled=True)]
    dot_general x6 -> x0, matrix products: 11.6 us -> none  [the longest x2 5.79 us: per_device(): jnp.einsum('kin,nkl->kil', slot_residual, slot_slopes, preferred_element_...]
    pallas_call x0 -> x3, Pallas kernels: none -> 11.6 us  [the longest x1 5.93 us: fit(): pl.pallas_call(functools.partial(fit_kernel, samp_dev), out_shape=[jax.Sh...]
    unnamed x10 -> x30, local copies, waits for them, and re-layouts: 1.02 us -> 12.6 us
    gather x4 -> x0, local copies, waits for them, and re-layouts: 10.5 us -> none  [the longest x2 7.15 us: per_device(): outgoing = jnp.take(local_rows, slope_all.reshape(-1), axis=1)]
    all_to_all x2 -> x1, starting transfers between devices: 11 us -> 7.3 us  [per_device(): lax.all_to_all(packed, 'samp', split_axis=0, concat_axis=0, tiled=True)]
    select_n x2, other arithmetic: 3.82 us -> 1.23 us  [the longest x1 1.22 us: own_places(): jnp.where(live, jnp.where(start >= 0, offset, ranked), -1).astype(jnp.int32)]
    reshape x2 -> x0, local copies, waits for them, and re-layouts: 2.38 us -> none  [per_device(): outgoing = outgoing.reshape(samp_dev, samp_count, need_count, block_size)]
  transfers between devices with their start and end apart: 2 -> 1, of which waited for: 2 -> 1; matrix products, arithmetic and copies ran while one was open for 9% -> 8% of each run, Pallas kernels for 0% -> 3%
where the time goes in v1:
time: 60 us; the launch traced here: 59.4 us
  waiting for transfers between devices  20.8 us (35%)
  local copies, waits for them, and re-layouts  14.5 us (24%)
  Pallas kernels  11.6 us (19%)
  starting transfers between devices  7.3 us (12%)
  other arithmetic  3.97 us (7%)
  between operations  1.32 us (2%)
    all_to_all x1, waiting for transfers between devices, per_device(): lax.all_to_all(packed, 'samp', split_axis=0, concat_axis=0, tiled=True)  20.8 us
    unnamed x30, local copies, waits for them, and re-layouts  12.6 us
    all_to_all x1, starting transfers between devices, per_device(): lax.all_to_all(packed, 'samp', split_axis=0, concat_axis=0, tiled=True)  7.3 us
    pallas_call x1, Pallas kernels, fit(): pl.pallas_call(functools.partial(fit_kernel, samp_dev), out_shape=[jax.Sh...  5.93 us
    pallas_call x1, Pallas kernels, pack(): pl.pallas_call(pack_kernel, out_shape=jax.ShapeDtypeStruct((devices, tall...  3.89 us
    pallas_call x1, Pallas kernels, stage(): pl.pallas_call(functools.partial(stage_kernel, rate, samp_dev), out_shape...  1.75 us
    select_n x1, other arithmetic, own_places(): jnp.where(live, jnp.where(start >= 0, offset, ranked), -1).astype(jnp.int32)  1.22 us
  transfers between devices with their start and end apart: 1, of which 1 were waited for; matrix products, arithmetic and copies ran while one was open for 8% of the time, Pallas kernels for 3%

profile of v1, /device:TPU:0, one launch (start us, length us, event | category | flops | bytes accessed | tf_op | source)
XLA Modules:
  0.0 59.4 jit_solution(5556508891598416258)
XLA Ops:
  0.6 1.0 %select_reduce_fusion.4 = (s32[32]{0:T(128)S(1)}, s32[32]{0:T(128)S(1)}, s32[32]{0:T(128)S(1)}, s32[32]{0:T(128)S(1)}) fusion(s32[32]{0:T(128)} %bitcast.19, s32[1,32,32]{2,1,0:T(8,128)} %param.10), kind=kLoop, calls=%fused_computation.9 | loop fusion | flops 13184 | bytes 4736 | tf_op jit(solution)/shard_map/reduce_max | solution.py:23
  1.6 0.0 copy-start.6
  1.6 1.1 %copy-done.6 = bf16[2,4,37632]{2,1,0:T(4,128)(2,1)S(1)} copy-done((bf16[2,4,37632]{2,1,0:T(4,128)(2,1)S(1)}, bf16[2,4,37632]{2,1,0:T(4,128)(2,1)}, u32[]{:S(2)}) %copy-start.6) | copy-done | bytes 602136
  2.7 0.0 copy-start.12
  2.7 0.7 %copy-done.12 = s32[1,32,32]{2,1,0:T(8,128)S(1)} copy-done((s32[1,32,32]{2,1,0:T(8,128)S(1)}, s32[1,32,32]{2,1,0:T(8,128)}, u32[]{:S(2)}) %copy-start.12) | copy-done | bytes 4120
  3.4 0.0 copy-start.13
  3.4 0.7 %copy-done.13 = s32[1,32]{1,0:T(1,128)S(1)} copy-done((s32[1,32]{1,0:T(1,128)S(1)}, s32[1,32]{1,0:T(1,128)}, u32[]{:S(2)}) %copy-start.13) | copy-done | bytes 152
  4.0 0.0 copy-start.14
  4.1 0.0 copy-start
  4.1 0.0 copy-start.11
  4.1 3.9 %pack_windows.1 = bf16[32,8,2560]{2,1,0:T(8,128)(2,1)S(1)} custom-call(s32[32]{0:T(128)S(1)} %compare_select_fusion.3.starts, s32[32,32]{1,0:T(8,128)S(1)} %bitcast.18, s32[32]{0:T(128)S(1)} %bitcast.20, bf16[2,4,37632]{2,1,0:T(4,128)(2,1)S(1)} %copy-done.6), custom_call_target="tpu_custom_call" | custom-call | tf_op jit(solution)/shard_map/pack_windows/pallas_call | solution.py:123
  8.0 0.0 copy-start.1
  8.0 1.0 %copy-done.1 = bf16[32,8,2560]{2,1,0:T(8,128)(2,1)} copy-done((bf16[32,8,2560]{2,1,0:T(8,128)(2,1)}, bf16[32,8,2560]{2,1,0:T(8,128)(2,1)S(1)}, u32[]{:S(2)}) %copy-start.1) | copy-done | bytes 1310744
  9.0 7.3 %all-to-all-start = ((bf16[32,8,2560]{2,1,0:T(8,128)(2,1)}), bf16[32,8,2560]{2,1,0:T(8,128)(2,1)S(1)}, u32[]{:S(2)}, u32[]{:S(2)}) async-start(bf16[32,8,2560]{2,1,0:T(8,128)(2,1)} %copy-done.1), calls=%async_computation | async-start | bytes 2621440 | tf_op jit(solution)/shard_map/all_to_all | solution.py:327
  16.3 0.0 copy-done.14
  16.3 0.6 constant_dynamic-slice_fusion.2
  16.9 0.6 dynamic_slice.15
  18.1 0.7 %iota_compare_fusion.2 = pred[32]{0:T(512)(128)(4,1)S(1)} fusion(s32[]{:T(128)} %bitcast), kind=kLoop, calls=%fused_computation.24 | loop fusion | flops 32 | bytes 36 | tf_op jit(solution)/shard_map/lt | solution.py:35
  18.7 0.7 %fusion.3 = (s32[32]{0:T(128)S(1)}, s32[32]{0:T(128)S(1)}) fusion(s32[1,32,32]{2,1,0:T(8,128)} %param.10, s32[]{:T(128)S(6)} %select_n.54, s32[1,32,32]{2,1,0:T(8,128)} %param.9), kind=kLoop, calls=%fused_computation.22 | loop fusion | bytes 516 | tf_op jit(solution)/shard_map/jit(dynamic_index_in_dim)/squeeze | solution.py:330
  19.4 0.2 fusion.2
  19.6 0.7 %not_and_fusion = pred[32]{0:T(512)(128)(4,1)S(1)} fusion(pred[32]{0:T(512)(128)(4,1)S(1)} %fusion.2, s32[]{:T(128)} %bitcast), kind=kLoop, calls=%fused_computation.14 | loop fusion | flops 96 | bytes 68 | tf_op jit(solution)/shard_map/and | solution.py:38
  20.3 0.1 convert_reduce_fusion
  20.4 0.2 select_reduce_fusion
  20.6 1.2 %fusion.5.places = s32[32]{0:T(128)S(1)} fusion(s32[32]{0:T(128)S(1)} %select_reduce_fusion, s32[32]{0:T(128)S(1)} %get-tuple-element.18, pred[]{:T(512)S(6)} %ge.11, s32[]{:T(128)} %bitcast.3, s32[]{:T(128)} %bitcast), kind=kLoop, calls=%fused_computation.25 | loop fusion | flops 224 | bytes 393 | tf_op jit(solution)/shard_map/jit(_where)/select_n | solution.py:43
  21.8 0.0 copy-done
  21.8 0.0 copy-done.11
  21.8 1.7 %stage_weights.1 = (f32[256,2560]{1,0:T(8,128)S(1)}, bf16[256,2560]{1,0:T(8,128)(2,1)S(1)}, f32[2,256,256]{2,1,0:T(8,128)S(1)}, f32[2,8,2560]{2,1,0:T(8,128)S(1)}) custom-call(s32[32]{0:T(128)S(1)} %fusion.5.places, s32[32]{0:T(128)S(1)} %get-tuple-element.19.acts, f32[32,128,128]{2,1,0:T(8,128)S(1)} %bitcast.15, bf16[2,256,128]{2,1,0:T(8,128)(2,1)S(1)} %copy-done.11), custom_call_target="tpu_custom_call" | custom-call | flops 100000000 | bytes 9000000 | tf_op jit(solution)/shard_map/stage_weights/pallas_call | solution.py:178
  23.6 0.0 copy-start.2
  23.6 1.5 %copy-done.2 = f32[256,2560]{1,0:T(8,128)} copy-done((f32[256,2560]{1,0:T(8,128)}, f32[256,2560]{1,0:T(8,128)S(1)}, u32[]{:S(2)}) %copy-start.2) | copy-done | bytes 2621464
  25.1 0.0 copy-start.4
  25.1 1.1 %copy-done.4 = bf16[256,2560]{1,0:T(8,128)(2,1)} copy-done((bf16[256,2560]{1,0:T(8,128)(2,1)}, bf16[256,2560]{1,0:T(8,128)(2,1)S(1)}, u32[]{:S(2)}) %copy-start.4) | copy-done | bytes 1310744
  26.2 0.0 copy-start.7
  26.2 0.8 %copy-done.7 = f32[2,256,256]{2,1,0:T(8,128)} copy-done((f32[2,256,256]{2,1,0:T(8,128)}, f32[2,256,256]{2,1,0:T(8,128)S(1)}, u32[]{:S(2)}) %copy-start.7) | copy-done | bytes 524312
  27.0 0.0 copy-start.9
  27.0 0.7 %copy-done.9 = f32[2,8,2560]{2,1,0:T(8,128)} copy-done((f32[2,8,2560]{2,1,0:T(8,128)}, f32[2,8,2560]{2,1,0:T(8,128)S(1)}, u32[]{:S(2)}) %copy-start.9) | copy-done | bytes 163864
  27.7 20.8 %all-to-all-done = bf16[32,8,2560]{2,1,0:T(8,128)(2,1)S(1)} async-done(((bf16[32,8,2560]{2,1,0:T(8,128)(2,1)}), bf16[32,8,2560]{2,1,0:T(8,128)(2,1)S(1)}, u32[]{:S(2)}, u32[]{:S(2)}) %all-to-all-start) | async-done | bytes 1310752 | tf_op jit(solution)/shard_map/all_to_all | solution.py:327
  48.4 0.0 copy-start.3
  48.4 1.7 %copy-done.3 = f32[256,2560]{1,0:T(8,128)S(1)} copy-done((f32[256,2560]{1,0:T(8,128)S(1)}, f32[256,2560]{1,0:T(8,128)}, u32[]{:S(2)}) %copy-start.3) | copy-done | bytes 2621464
  50.2 0.0 copy-start.5
  50.2 1.3 %copy-done.5 = bf16[256,2560]{1,0:T(8,128)(2,1)S(1)} copy-done((bf16[256,2560]{1,0:T(8,128)(2,1)S(1)}, bf16[256,2560]{1,0:T(8,128)(2,1)}, u32[]{:S(2)}) %copy-start.5) | copy-done | bytes 1310744
  51.5 0.0 copy-start.8
  51.5 1.0 %copy-done.8 = f32[2,256,256]{2,1,0:T(8,128)S(1)} copy-done((f32[2,256,256]{2,1,0:T(8,128)S(1)}, f32[2,256,256]{2,1,0:T(8,128)}, u32[]{:S(2)}) %copy-start.8) | copy-done | bytes 524312
  52.5 0.0 copy-start.10
  52.5 0.9 %copy-done.10 = f32[2,8,2560]{2,1,0:T(8,128)S(1)} copy-done((f32[2,8,2560]{2,1,0:T(8,128)S(1)}, f32[2,8,2560]{2,1,0:T(8,128)}, u32[]{:S(2)}) %copy-start.10) | copy-done | bytes 163864
  53.5 5.9 %fit_steps.1 = (f32[32,128,128]{2,1,0:T(8,128)}, bf16[256,128]{1,0:T(8,128)(2,1)}) custom-call(s32[32]{0:T(128)S(1)} %fusion.5.places, s32[32]{0:T(128)S(1)} %get-tuple-element.19.acts, bf16[256,2560]{1,0:T(8,128)(2,1)S(1)} %bitcast.17, f32[256,2560]{1,0:T(8,128)S(1)} %copy-done.3, bf16[256,2560]{1,0:T(8,128)(2,1)S(1)} %copy-done.5, ...), custom_call_target="tpu_custom_call" | custom-call | tf_op jit(solution)/shard_map/fit_steps/pallas_call | solution.py:272
  (1 shorter events, 0.0 us)
Async XLA Ops:
  1.6 1.1 %copy-start.6 = (bf16[2,4,37632]{2,1,0:T(4,128)(2,1)S(1)}, bf16[2,4,37632]{2,1,0:T(4,128)(2,1)}, u32[]{:S(2)}) copy-start(bf16[2,4,37632]{2,1,0:T(4,128)(2,1)} %slopes.1) | copy-start | bytes 1806340
  2.7 0.7 %copy-start.12 = (s32[1,32,32]{2,1,0:T(8,128)S(1)}, s32[1,32,32]{2,1,0:T(8,128)}, u32[]{:S(2)}) copy-start(s32[1,32,32]{2,1,0:T(8,128)} %param.10) | copy-start | bytes 12292
  3.4 0.7 %copy-start.13 = (s32[1,32]{1,0:T(1,128)S(1)}, s32[1,32]{1,0:T(1,128)}, u32[]{:S(2)}) copy-start(s32[1,32]{1,0:T(1,128)} %param.11) | copy-start | bytes 388
  4.0 12.3 %copy-start.14 = (s32[1,32]{1,0:T(1,128)S(1)}, s32[1,32]{1,0:T(1,128)}, u32[]{:S(2)}) copy-start(s32[1,32]{1,0:T(1,128)} %param.11) | copy-start | bytes 388
  4.1 17.8 %copy-start = (f32[1,1,32,128,128]{4,3,2,1,0:T(8,128)S(1)}, f32[1,1,32,128,128]{4,3,2,1,0:T(8,128)}, u32[]{:S(2)}) copy-start(f32[1,1,32,128,128]{4,3,2,1,0:T(8,128)} %param.8) | copy-start | bytes 6291460
  4.1 17.8 %copy-start.11 = (bf16[2,256,128]{2,1,0:T(8,128)(2,1)S(1)}, bf16[2,256,128]{2,1,0:T(8,128)(2,1)}, u32[]{:S(2)}) copy-start(bf16[2,256,128]{2,1,0:T(8,128)(2,1)} %targets.1) | copy-start | bytes 393220
  8.0 1.1 %copy-start.1 = (bf16[32,8,2560]{2,1,0:T(8,128)(2,1)}, bf16[32,8,2560]{2,1,0:T(8,128)(2,1)S(1)}, u32[]{:S(2)}) copy-start(bf16[32,8,2560]{2,1,0:T(8,128)(2,1)S(1)} %pack_windows.1) | copy-start | bytes 3932164
  9.0 39.4 %all-to-all-start = ((bf16[32,8,2560]{2,1,0:T(8,128)(2,1)}), bf16[32,8,2560]{2,1,0:T(8,128)(2,1)S(1)}, u32[]{:S(2)}, u32[]{:S(2)}) async-start(bf16[32,8,2560]{2,1,0:T(8,128)(2,1)} %copy-done.1), calls=%async_computation | async-start | bytes 2621440 | tf_op jit(solution)/shard_map/all_to_all | solution.py:327
  23.6 1.5 %copy-start.2 = (f32[256,2560]{1,0:T(8,128)}, f32[256,2560]{1,0:T(8,128)S(1)}, u32[]{:S(2)}) copy-start(f32[256,2560]{1,0:T(8,128)S(1)} %get-tuple-element.8.stack_in) | copy-start | bytes 7864324
  25.1 1.1 %copy-start.4 = (bf16[256,2560]{1,0:T(8,128)(2,1)}, bf16[256,2560]{1,0:T(8,128)(2,1)S(1)}, u32[]{:S(2)}) copy-start(bf16[256,2560]{1,0:T(8,128)(2,1)S(1)} %get-tuple-element.9.low_in) | copy-start | bytes 3932164
  26.2 0.8 %copy-start.7 = (f32[2,256,256]{2,1,0:T(8,128)}, f32[2,256,256]{2,1,0:T(8,128)S(1)}, u32[]{:S(2)}) copy-start(f32[2,256,256]{2,1,0:T(8,128)S(1)} %get-tuple-element.10.spread) | copy-start | bytes 1572868
  27.0 0.7 %copy-start.9 = (f32[2,8,2560]{2,1,0:T(8,128)}, f32[2,8,2560]{2,1,0:T(8,128)S(1)}, u32[]{:S(2)}) copy-start(f32[2,8,2560]{2,1,0:T(8,128)S(1)} %get-tuple-element.11.rates) | copy-start | bytes 491524
  48.4 1.7 %copy-start.3 = (f32[256,2560]{1,0:T(8,128)S(1)}, f32[256,2560]{1,0:T(8,128)}, u32[]{:S(2)}) copy-start(f32[256,2560]{1,0:T(8,128)} %copy-done.2) | copy-start | bytes 7864324
  50.2 1.3 %copy-start.5 = (bf16[256,2560]{1,0:T(8,128)(2,1)S(1)}, bf16[256,2560]{1,0:T(8,128)(2,1)}, u32[]{:S(2)}) copy-start(bf16[256,2560]{1,0:T(8,128)(2,1)} %copy-done.4) | copy-start | bytes 3932164
  51.5 1.0 %copy-start.8 = (f32[2,256,256]{2,1,0:T(8,128)S(1)}, f32[2,256,256]{2,1,0:T(8,128)}, u32[]{:S(2)}) copy-start(f32[2,256,256]{2,1,0:T(8,128)} %copy-done.7) | copy-start | bytes 1572868
  52.5 0.9 %copy-start.10 = (f32[2,8,2560]{2,1,0:T(8,128)S(1)}, f32[2,8,2560]{2,1,0:T(8,128)}, u32[]{:S(2)}) copy-start(f32[2,8,2560]{2,1,0:T(8,128)} %copy-done.9) | copy-start | bytes 491524

commit v2 on v0

v2 whole, which is shorter than its diff:
```python
import functools

import jax
import jax.numpy as jnp
from jax import lax
from jax.experimental import pallas as pl
from jax.experimental.pallas import tpu as pltpu
from jax.sharding import PartitionSpec as P

STEPS = 2
DISTINCT = 20
BLOCK = 128
MIB = 1 << 20


def own_places(blocks_own, count_own, groups):
    ids = jnp.arange(blocks_own.shape[0])
    half = groups // 2
    turned = jnp.where(blocks_own >= groups - half, blocks_own - (groups - half), blocks_own + half)
    straight = blocks_own - jnp.min(blocks_own)
    around = turned - jnp.min(turned)
    same = blocks_own[:, None] == blocks_own[None, :]
    before = ids[None, :] < ids[:, None]
    first = ~jnp.any(same & before, axis=1)
    rank = jnp.sum(first[None, :] & before, axis=1)
    ranked = jnp.sum(jnp.where(same & first[None, :], rank[None, :], 0), axis=1)
    place = jnp.where(
        jnp.max(straight) < DISTINCT, straight, jnp.where(jnp.max(around) < DISTINCT, around, ranked)
    )
    return jnp.where(ids < count_own, place, -1).astype(jnp.int32)


def pack_kernel(
    pieces, blocks_hbm, slopes, out, blocks_of, raw, rows, row_starts, starts, table, sems, load_sems, small_sems
):
    steps, samp_dev, width = slopes.shape
    groups = width // BLOCK
    devices, _, window = out.shape
    edges = [groups * i // pieces for i in range(pieces + 1)]

    def load(i):
        cols = pl.ds(edges[i] * BLOCK, (edges[i + 1] - edges[i]) * BLOCK)
        return pltpu.make_async_copy(slopes.at[:, :, cols], raw.at[:, :, cols], load_sems.at[i])

    to_vectors = pltpu.make_async_copy(blocks_hbm, blocks_of, small_sems.at[0])
    to_vectors.start()
    for i in range(pieces):
        load(i).start()
    to_vectors.wait()
    blocks = blocks_of[...].astype(jnp.float32)
    half = groups // 2
    turned = jnp.where(blocks >= groups - half, blocks - (groups - half), blocks + half)

    def span(named):
        low = jnp.min(named, axis=1, keepdims=True)
        return low, jnp.max(named, axis=1, keepdims=True) - low < DISTINCT

    low, fits = span(blocks)
    low_turned, fits_turned = span(turned)
    unturned = jnp.where(low_turned >= half, low_turned - half, low_turned + (groups - half))
    first = jnp.where(fits, low, jnp.where(fits_turned, unturned, -1.0))
    lane = lax.broadcasted_iota(jnp.int32, (devices, BLOCK), 1)
    device = lax.broadcasted_iota(jnp.int32, (devices, BLOCK), 0)
    row = jnp.sum(jnp.where(lane == device, jnp.broadcast_to(first, (devices, BLOCK)), 0.0), axis=0, keepdims=True)
    least = jnp.min(row, axis=1, keepdims=True)
    last_lane = lax.broadcasted_iota(jnp.int32, (1, BLOCK), 1) == BLOCK - 1
    row_starts[...] = jnp.where(last_lane, least, row).astype(jnp.int32)
    to_scalars = pltpu.make_async_copy(row_starts, starts, small_sems.at[1])
    to_scalars.start()

    def join(first, last):
        cols = slice(first * BLOCK, last * BLOCK)
        return jnp.concatenate([raw[t, :, cols] for t in range(steps)], axis=0)

    span_blocks = window // BLOCK
    for i in range(pieces):
        load(i).wait()
        for at in range(edges[i], edges[i + 1], 7):
            end = min(at + 7, edges[i + 1])
            rows[:, at * BLOCK : end * BLOCK] = join(at, end)
        if i == 0:
            rows[:, width:] = rows[:, :window]
    to_scalars.wait()

    def to_device(d, group, at, count):
        return pltpu.make_async_copy(
            rows.at[:, pl.ds(pl.multiple_of(group * BLOCK, BLOCK), count * BLOCK)],
            out.at[d, :, pl.ds(pl.multiple_of(at * BLOCK, BLOCK), count * BLOCK)],
            sems.at[d],
        )

    @pl.when(starts[0, BLOCK - 1] >= 0)
    def _():
        for d in range(devices):
            to_device(d, starts[0, d], 0, span_blocks).start()

    @pl.when(starts[0, BLOCK - 1] < 0)
    def _():
        copy_table = pltpu.make_async_copy(blocks_of, table, small_sems.at[2])
        copy_table.start()
        copy_table.wait()

        def one_by_one(d):
            def slot(k, placed):
                group = table[d, k]
                seen = lax.fori_loop(0, k, lambda j, s: jnp.where(table[d, j] == group, 1, s), jnp.int32(0))

                @pl.when(seen == 0)
                def _():
                    to_device(d, group, placed, 1).start()

                return placed + 1 - seen

            placed = lax.fori_loop(0, blocks_of.shape[1], slot, jnp.int32(0))

            def fill(j, carry):
                to_device(d, table[d, 0], j, 1).start()
                return carry

            lax.fori_loop(placed, span_blocks, fill, 0)

        def send(d, carry):
            @pl.when(starts[0, d] >= 0)
            def _():
                to_device(d, starts[0, d], 0, span_blocks).start()

            @pl.when(starts[0, d] < 0)
            def _():
                one_by_one(d)

            return carry

        lax.fori_loop(0, devices, send, 0)

    for d in range(devices):
        to_device(d, 0, 0, span_blocks).wait()


def pack(blocks_of, slopes, pieces=3):
    steps, samp_dev, width = slopes.shape
    devices, slots = blocks_of.shape
    tall = steps * samp_dev
    window = DISTINCT * BLOCK
    return pl.pallas_call(
        functools.partial(pack_kernel, pieces),
        out_shape=pltpu.HBM((devices, tall, window), slopes.dtype),
        in_specs=[pl.BlockSpec(memory_space=pltpu.HBM)] * 2,
        out_specs=pl.BlockSpec(memory_space=pltpu.HBM),
        scratch_shapes=[
            pltpu.VMEM((devices, slots), jnp.int32),
            pltpu.VMEM(slopes.shape, slopes.dtype),
            pltpu.VMEM((tall, width + window), slopes.dtype),
            pltpu.VMEM((1, BLOCK), jnp.int32),
            pltpu.SMEM((1, BLOCK), jnp.int32),
            pltpu.SMEM((devices, slots), jnp.int32),
            pltpu.SemaphoreType.DMA((devices,)),
            pltpu.SemaphoreType.DMA((pieces,)),
            pltpu.SemaphoreType.DMA((3,)),
        ],
        compiler_params=pltpu.CompilerParams(vmem_limit_bytes=16 * MIB),
        name="pack_windows",
    )(pltpu.with_memory_space_constraint(blocks_of, pltpu.HBM), pltpu.with_memory_space_constraint(slopes, pltpu.HBM))


def spreader(samples, wide, samp_dev, step, dtype):
    tall = wide * samp_dev // samples
    n = lax.broadcasted_iota(jnp.int32, (samples, wide), 0)
    c = lax.broadcasted_iota(jnp.int32, (samples, wide), 1)
    column = (n // samp_dev) * tall + step * samp_dev + n % samp_dev
    return (c == column).astype(jnp.float32).astype(dtype)


def fit_kernel(step_rate, samp_dev, holder, seen, weights, targets_hbm, fitted, residual, targets, stack, low, in_sem, out_sems):
    steps, rows, samples = targets.shape
    slots, block, _ = weights.shape
    wide, window = seen.shape
    span = window // block
    blocks = rows // block
    cells = blocks * span
    tall = wide * samp_dev // samples

    load = pltpu.make_async_copy(targets_hbm, targets, in_sem)
    load.start()

    def keep(k, carry):
        pltpu.make_async_copy(weights.at[k], fitted.at[k], out_sems.at[k]).start()
        return carry

    lax.fori_loop(holder[cells], slots, keep, 0)

    def at_rows(a):
        return slice(a * block, (a + 1) * block)

    def at_cols(p):
        return slice(p * block, (p + 1) * block)

    def held(a, p):
        slot = holder[a * span + p]
        return jnp.where(slot >= 0, weights[jnp.maximum(slot, 0)], 0.0)

    for p in range(span):
        for a in range(blocks):
            low[at_rows(a), at_cols(p)] = held(a, p).astype(low.dtype)

    column = lax.broadcasted_iota(jnp.int32, (rows, wide), 1)
    step_of = (column % tall) // samp_dev
    chunk = 4
    for t in range(steps):
        predicted = lax.dot_general(
            low[...], seen[...], (((1,), (1,)), ((), ())), preferred_element_type=jnp.float32
        )
        if t == 0:
            load.wait()
        pick = spreader(samples, wide, samp_dev, t, jnp.bfloat16)
        wanted = jnp.dot(targets[t], pick, preferred_element_type=jnp.float32)
        rest = jnp.where(step_of == t, predicted - wanted, 0.0).astype(jnp.bfloat16)
        if t == steps - 1:
            residual[...] = lax.dot_general(
                rest, pick, (((1,), (1,)), ((), ())), preferred_element_type=jnp.float32
            ).astype(residual.dtype)
        for first in range(0, span, chunk):
            last = min(first + chunk, span)
            gradient = jnp.dot(rest, seen[:, first * block : last * block], preferred_element_type=jnp.float32)
            cell_list = [(a, p) for p in range(first, last) for a in range(blocks)]
            for a, p in cell_list:
                j = a * span + p
                rate = jnp.where(holder[j] >= 0, jnp.float32(step_rate), jnp.float32(0))
                old = held(a, p) if t == 0 else stack[j]
                new = old - rate * gradient[at_rows(a), at_cols(p - first)]
                stack[j] = new
                if t < steps - 1:
                    low[at_rows(a), at_cols(p)] = new.astype(low.dtype)
            if t == steps - 1:
                for a, p in cell_list:
                    j = a * span + p
                    slot = holder[j]

                    @pl.when(slot >= 0)
                    def _(j=j, slot=slot):
                        pltpu.make_async_copy(stack.at[j], fitted.at[slot], out_sems.at[slot]).start()

    def settle(k, carry):
        pltpu.make_async_copy(stack.at[0], fitted.at[k], out_sems.at[k]).wait()
        return carry

    lax.fori_loop(0, slots, settle, 0)


def fit(step_rate, samp_dev, holder, seen, weights, targets):
    steps, rows, samples = targets.shape
    slots, block, _ = weights.shape
    window = seen.shape[1]
    cells = rows // block * DISTINCT
    smem = pl.BlockSpec(memory_space=pltpu.SMEM)
    vmem = pl.BlockSpec(memory_space=pltpu.VMEM)
    hbm = pl.BlockSpec(memory_space=pltpu.HBM)
    return pl.pallas_call(
        functools.partial(fit_kernel, step_rate, samp_dev),
        out_shape=[
            pltpu.HBM(weights.shape, jnp.float32),
            jax.ShapeDtypeStruct((rows, samples), jnp.bfloat16),
        ],
        in_specs=[smem, vmem, vmem, hbm],
        out_specs=[hbm, vmem],
        scratch_shapes=[
            pltpu.VMEM(targets.shape, targets.dtype),
            pltpu.VMEM((cells, block, block), jnp.float32),
            pltpu.VMEM((rows, window), jnp.bfloat16),
            pltpu.SemaphoreType.DMA,
            pltpu.SemaphoreType.DMA((slots,)),
        ],
        compiler_params=pltpu.CompilerParams(vmem_limit_bytes=24 * MIB),
        name="fit_steps",
    )(holder, seen, weights, pltpu.with_memory_space_constraint(targets, pltpu.HBM))


def fit_over_groups(step_rate, samp_dev, places, acts, arrived, weights, targets):
    steps, rows, samples = targets.shape
    slots, block, _ = weights.shape
    live = places >= 0
    devices = arrived.shape[0]
    grouped = arrived.reshape(devices, steps, samp_dev, DISTINCT, block)
    slot_slopes = jnp.take(grouped, jnp.maximum(places, 0), axis=3)
    blocks = rows // block
    onehot = ((acts[None, :] == jnp.arange(blocks)[:, None]) & live[None, :]).astype(jnp.float32)
    residual = None
    for t in range(steps):
        now = slot_slopes[:, t].reshape(samples, slots, block)
        partial_sums = jnp.einsum(
            "kil,nkl->kin", weights.astype(jnp.bfloat16), now, preferred_element_type=jnp.float32
        )
        summed = jnp.einsum("jk,kin->jin", onehot, partial_sums, precision=lax.Precision.HIGHEST)
        total = lax.psum(summed, "sens")
        residual = (total - targets[t].reshape(blocks, block, samples)).astype(jnp.bfloat16)
        gradient = jnp.einsum(
            "kin,nkl->kil", jnp.take(residual, acts, axis=0), now, preferred_element_type=jnp.float32
        )
        weights = jnp.where(live[:, None, None], weights - step_rate * gradient, weights)
    return weights, residual.reshape(rows, samples)


def per_device(slopes, targets, reconstructor, foot_act, foot_slope, foot_count):
    own_index = lax.axis_index("samp")
    block = reconstructor.shape[-1]
    slots = reconstructor.shape[2]
    groups = slopes.shape[2] // block
    samp_dev = slopes.shape[1]
    samples = targets.shape[2]
    devices = foot_slope.shape[1]
    cells = targets.shape[1] // block * DISTINCT
    step_rate = slots * block / (samples + 3 * slots * block)
    packed = pack(foot_slope[0], slopes)
    arrived = lax.all_to_all(packed, "samp", split_axis=0, concat_axis=0, tiled=True)

    def own(table):
        return lax.dynamic_index_in_dim(table, own_index, 0, keepdims=False)

    count = own(foot_count[0])
    places = own_places(own(foot_slope[0]), count, groups)
    acts = own(foot_act[0])
    weights = reconstructor[0, 0]
    if lax.axis_size("sens") > 1:
        fitted, residual = fit_over_groups(step_rate, samp_dev, places, acts, arrived, weights, targets)
        return fitted[None, None], residual
    cell = jnp.where(places >= 0, acts * DISTINCT + places, -1)
    held = cell[None, :] == jnp.arange(cells)[:, None]
    holder = jnp.sum(jnp.where(held, jnp.arange(slots)[None, :] + 1, 0), axis=1) - 1
    holder = jnp.concatenate([holder, count[None]]).astype(jnp.int32)
    seen = arrived.reshape(devices * STEPS * samp_dev, DISTINCT * block)
    fitted, residual = fit(step_rate, samp_dev, holder, seen, weights, targets)
    return fitted[None, None], residual


def solution(mesh):
    return jax.shard_map(
        per_device,
        mesh=mesh,
        in_specs=(
            P(None, "samp", "sens"),
            P(None, "samp", None),
            P("sens", "samp", None, None, None),
            P("sens", None, None),
            P("sens", None, None),
            P("sens", None),
        ),
        out_specs=(P("sens", "samp", None, None, None), P("samp", None)),
        check_vma=False,
    )
```

time: 93.5 us -> 48.9 us (0.52)
  waiting for transfers between devices: 43.1 us -> 21.7 us
  local copies, waits for them, and re-layouts: 21.2 us -> 0.59 us
  matrix products: 11.6 us -> 0 us
  Pallas kernels: 0 us -> 8.38 us
  starting transfers between devices: 11 us -> 7.3 us
  other arithmetic: 5.24 us -> 8.59 us
  between operations: 0.81 us -> 1.96 us
    all_to_all x2 -> x1, waiting for transfers between devices: 43.1 us -> 21.7 us  [per_device(): lax.all_to_all(packed, 'samp', split_axis=0, concat_axis=0, tiled=True)]
    dot_general x6 -> x0, matrix products: 11.6 us -> none  [the longest x2 5.79 us: per_device(): jnp.einsum('kin,nkl->kil', slot_residual, slot_slopes, preferred_element_...]
    gather x4 -> x0, local copies, waits for them, and re-layouts: 10.5 us -> none  [the longest x2 7.15 us: per_device(): outgoing = jnp.take(local_rows, slope_all.reshape(-1), axis=1)]
    pallas_call x0 -> x2, Pallas kernels: none -> 8.38 us  [the longest x1 5.23 us: fit(): pl.pallas_call(functools.partial(fit_kernel, step_rate, samp_dev), out_sh...]
    all_to_all x2 -> x1, starting transfers between devices: 11 us -> 7.3 us  [per_device(): lax.all_to_all(packed, 'samp', split_axis=0, concat_axis=0, tiled=True)]
    reduce_min x0 -> x2, other arithmetic: none -> 2.73 us  [the longest x1 1.41 us: own_places(): around = turned - jnp.min(turned)]
    reshape x2 -> x0, local copies, waits for them, and re-layouts: 2.38 us -> none  [per_device(): outgoing = outgoing.reshape(samp_dev, samp_count, need_count, block_size)]
    dot_general x1 -> x0, local copies, waits for them, and re-layouts: 2.37 us -> none  [per_device(): jnp.einsum('kil,nkl->kin', weights_low, slot_slopes, preferred_element_ty...]
  transfers between devices with their start and end apart: 2 -> 1, of which waited for: 2 -> 1; matrix products, arithmetic and copies ran while one was open for 9% -> 19% of each run, Pallas kernels for 0% -> 0%
where the time goes in v2:
time: 48.9 us; the launch traced here: 48.5 us
  waiting for transfers between devices  21.7 us (44%)
  other arithmetic  8.59 us (18%)
  Pallas kernels  8.38 us (17%)
  starting transfers between devices  7.3 us (15%)
  between operations  1.96 us (4%)
  local copies, waits for them, and re-layouts  0.59 us (1%)
    all_to_all x1, waiting for transfers between devices, per_device(): lax.all_to_all(packed, 'samp', split_axis=0, concat_axis=0, tiled=True)  21.7 us
    all_to_all x1, starting transfers between devices, per_device(): lax.all_to_all(packed, 'samp', split_axis=0, concat_axis=0, tiled=True)  7.3 us
    pallas_call x1, Pallas kernels, fit(): pl.pallas_call(functools.partial(fit_kernel, step_rate, samp_dev), out_sh...  5.23 us
    pallas_call x1, Pallas kernels, pack(): pl.pallas_call(functools.partial(pack_kernel, pieces), out_shape=pltpu.HB...  3.15 us
    select_n x1, other arithmetic, per_device(): cell = jnp.where(places >= 0, acts * DISTINCT + places, -1)  2.6 us
    reduce_max x1, other arithmetic, own_places(): jnp.max(straight) < DISTINCT  1.95 us
    reduce_min x1, other arithmetic, own_places(): around = turned - jnp.min(turned)  1.41 us
    reduce_min x1, other arithmetic, own_places(): straight = blocks_own - jnp.min(blocks_own)  1.32 us
  transfers between devices with their start and end apart: 1, of which 1 were waited for; matrix products, arithmetic and copies ran while one was open for 19% of the time, Pallas kernels for 0%

profile of v2, /device:TPU:0, one launch (start us, length us, event | category | flops | bytes accessed | tf_op | source)
XLA Modules:
  0.0 48.5 jit_solution(7776147173496888220)
XLA Ops:
  0.6 0.0 copy-start
  0.6 0.0 copy-start.1
  0.7 3.2 %pack_windows.1 = bf16[32,8,2560]{2,1,0:T(8,128)(2,1)} custom-call(s32[32,32]{1,0:T(8,128)} %bitcast.17, bf16[2,4,37632]{2,1,0:T(4,128)(2,1)} %slopes.1), custom_call_target="tpu_custom_call" | custom-call | tf_op jit(solution)/shard_map/pack_windows/pallas_call | solution.py:144
  3.8 7.3 %all-to-all-start = ((bf16[32,8,2560]{2,1,0:T(8,128)(2,1)}), bf16[32,8,2560]{2,1,0:T(8,128)(2,1)S(1)}, u32[]{:S(2)}, u32[]{:S(2)}) async-start(bf16[32,8,2560]{2,1,0:T(8,128)(2,1)} %pack_windows.1), calls=%async_computation | async-start | bytes 2621440 | tf_op jit(solution)/shard_map/all_to_all | solution.py:313
  11.1 1.3 %fusion.5 = s32[]{:T(128)} fusion(s32[1,32,32]{2,1,0:T(8,128)} %param.10, s32[]{:T(128)S(6)} %select_n.60), kind=kLoop, calls=%fused_computation.25 | loop fusion | flops 31 | bytes 136 | tf_op jit(solution)/shard_map/reduce_min | solution.py:20
  12.5 0.0 copy-done
  12.5 0.6 %constant_dynamic-slice_fusion.2 = s32[1,1]{1,0:T(1,128)} fusion(s32[1,32]{1,0:T(1,128)S(1)} %copy-done, s32[]{:T(128)S(6)} %select_n.60), kind=kLoop, calls=%fused_computation.16 | loop fusion | bytes 12 | tf_op jit(solution)/shard_map/jit(dynamic_index_in_dim)/dynamic_slice | solution.py:316
  13.0 1.4 %fusion.7 = (s32[]{:T(128)}, s32[32]{0:T(128)S(1)}) fusion(s32[1,32,32]{2,1,0:T(8,128)} %param.10, s32[]{:T(128)S(6)} %select_n.60), kind=kLoop, calls=%fused_computation.27 | loop fusion | flops 159 | bytes 264 | tf_op jit(solution)/shard_map/reduce_min | solution.py:21
  14.4 0.2 fusion.1
  14.6 2.0 %subtract_reduce_fusion.1 = (s32[]{:T(128)}, s32[]{:T(128)}) fusion(s32[32]{0:T(128)S(1)} %get-tuple-element.9, s32[]{:T(128)} %fusion.5, s32[]{:T(128)} %get-tuple-element.8), kind=kLoop, calls=%fused_computation.23 | loop fusion | flops 254 | bytes 144 | tf_op jit(solution)/shard_map/reduce_max | solution.py:28
  17.9 0.1 convert_reduce_fusion
  18.0 0.2 select_reduce_fusion.1
  18.2 2.6 %compare_select_fusion = s32[32]{0:T(128)S(1)} fusion(s32[1,32,32]{2,1,0:T(8,128)} %param.9, s32[]{:T(128)S(6)} %select_n.60, s32[32]{0:T(128)S(1)} %select_reduce_fusion.1, pred[]{:T(512)S(6)} %lt.46, pred[]{:T(512)S(6)} %lt.45, s32[32]{0:T(128)S(1)} %get-tuple-element.9, s32[]{:T(128)} %get-tuple-element.8, s32[]{:T(128)} %fusion.5, s32[]{:T(128)} %bitcast), kind=kLoop, calls=%fused_computation.9 | loop fusion | flops 448 | bytes 530 | tf_op jit(solution)/shard_map/jit(_where)/select_n | solution.py:325
  20.8 0.1 select_reduce_fusion
  20.9 0.7 %pad_add_fusion.holder = s32[41]{0:T(128)S(1)} fusion(s32[1]{0:T(128)} %bitcast.3, s32[40]{0:T(128)S(1)} %broadcast_add_fusion), kind=kLoop, calls=%fused_computation.20 | loop fusion | flops 41 | bytes 328 | tf_op jit(solution)/shard_map/concatenate | solution.py:328
  21.6 21.7 %all-to-all-done = bf16[32,8,2560]{2,1,0:T(8,128)(2,1)S(1)} async-done(((bf16[32,8,2560]{2,1,0:T(8,128)(2,1)}), bf16[32,8,2560]{2,1,0:T(8,128)(2,1)S(1)}, u32[]{:S(2)}, u32[]{:S(2)}) %all-to-all-start) | async-done | bytes 1310752 | tf_op jit(solution)/shard_map/all_to_all | solution.py:313
  43.3 0.0 copy-done.1
  43.3 5.2 %fit_steps.1 = (f32[32,128,128]{2,1,0:T(8,128)}, bf16[256,128]{1,0:T(8,128)(2,1)}) custom-call(s32[41]{0:T(128)S(1)} %pad_add_fusion.holder, bf16[256,2560]{1,0:T(8,128)(2,1)S(1)} %bitcast.15, f32[32,128,128]{2,1,0:T(8,128)S(1)} %bitcast.16, bf16[2,256,128]{2,1,0:T(8,128)(2,1)} %targets_hbm.1), custom_call_target="tpu_custom_call" | custom-call | tf_op jit(solution)/shard_map/fit_steps/pallas_call | solution.py:257
  (3 shorter events, 0.0 us)
Async XLA Ops:
  0.6 11.8 %copy-start = (s32[1,32]{1,0:T(1,128)S(1)}, s32[1,32]{1,0:T(1,128)}, u32[]{:S(2)}) copy-start(s32[1,32]{1,0:T(1,128)} %param.11) | copy-start | bytes 388
  0.6 42.6 %copy-start.1 = (f32[1,1,32,128,128]{4,3,2,1,0:T(8,128)S(1)}, f32[1,1,32,128,128]{4,3,2,1,0:T(8,128)}, u32[]{:S(2)}) copy-start(f32[1,1,32,128,128]{4,3,2,1,0:T(8,128)} %param.8) | copy-start | bytes 6291460
  3.8 39.4 %all-to-all-start = ((bf16[32,8,2560]{2,1,0:T(8,128)(2,1)}), bf16[32,8,2560]{2,1,0:T(8,128)(2,1)S(1)}, u32[]{:S(2)}, u32[]{:S(2)}) async-start(bf16[32,8,2560]{2,1,0:T(8,128)(2,1)} %pack_windows.1), calls=%async_computation | async-start | bytes 2621440 | tf_op jit(solution)/shard_map/all_to_all | solution.py:313

commit v3 on v2

v3 whole, which is shorter than its diff:
```python
import functools

import jax
import jax.numpy as jnp
from jax import lax
from jax.experimental import pallas as pl
from jax.experimental.pallas import tpu as pltpu
from jax.sharding import PartitionSpec as P

STEPS = 2
DISTINCT = 20
BLOCK = 128
MIB = 1 << 20


def own_places(blocks_own, count_own, groups):
    ids = jnp.arange(blocks_own.shape[0])
    half = groups // 2
    turned = jnp.where(blocks_own >= groups - half, blocks_own - (groups - half), blocks_own + half)
    straight = blocks_own - jnp.min(blocks_own)
    around = turned - jnp.min(turned)
    same = blocks_own[:, None] == blocks_own[None, :]
    before = ids[None, :] < ids[:, None]
    first = ~jnp.any(same & before, axis=1)
    rank = jnp.sum(first[None, :] & before, axis=1)
    ranked = jnp.sum(jnp.where(same & first[None, :], rank[None, :], 0), axis=1)
    place = jnp.where(
        jnp.max(straight) < DISTINCT, straight, jnp.where(jnp.max(around) < DISTINCT, around, ranked)
    )
    return jnp.where(ids < count_own, place, -1).astype(jnp.int32)


def pack_kernel(pieces, blocks_hbm, slopes, out, blocks_of, rows, starts, table, sems, load_sems, table_sems):
    steps, samp_dev, width = slopes.shape
    groups = width // BLOCK
    devices, _, window = out.shape
    span = window // BLOCK
    slots = blocks_of.shape[1]
    half = groups // 2

    read_table = pltpu.make_async_copy(blocks_hbm, blocks_of, table_sems.at[0])
    read_table.start()
    parts = [(groups * i // pieces, groups * (i + 1) // pieces, 0) for i in range(pieces)] + [(0, span, groups)]
    loads = []
    for i, (first, last, shift) in enumerate(parts):
        for t in range(steps):
            source = slopes.at[t, :, pl.ds(first * BLOCK, (last - first) * BLOCK)]
            target = rows.at[pl.ds(t * samp_dev, samp_dev), pl.ds((first + shift) * BLOCK, (last - first) * BLOCK)]
            loads.append(pltpu.make_async_copy(source, target, load_sems.at[i, t]))
    for load in loads:
        load.start()

    read_table.wait()
    blocks = blocks_of[...].astype(jnp.float32)
    turned = jnp.where(blocks >= groups - half, blocks - (groups - half), blocks + half)

    def extent(named):
        low = jnp.min(named, axis=1, keepdims=True)
        return low, jnp.max(named, axis=1, keepdims=True) - low < DISTINCT

    low, fits = extent(blocks)
    low_turned, fits_turned = extent(turned)
    unturned = jnp.where(low_turned >= half, low_turned - half, low_turned + (groups - half))
    first = jnp.where(fits, low, jnp.where(fits_turned, unturned, -1.0)).astype(jnp.int32)
    first_of = [first[d, 0] for d in range(devices)]
    least = functools.reduce(jnp.minimum, first_of)
    for load in loads:
        load.wait()

    def to_device(d, group, at, count):
        return pltpu.make_async_copy(
            rows.at[:, pl.ds(pl.multiple_of(group * BLOCK, BLOCK), count * BLOCK)],
            out.at[d, :, pl.ds(pl.multiple_of(at * BLOCK, BLOCK), count * BLOCK)],
            sems.at[d],
        )

    @pl.when(least >= 0)
    def _():
        for d in range(devices):
            to_device(d, first_of[d], 0, span).start()

    @pl.when(least < 0)
    def _():
        for d in range(devices):
            starts[d] = first_of[d]
        copy_table = pltpu.make_async_copy(blocks_of, table, table_sems.at[1])
        copy_table.start()
        copy_table.wait()

        def one_by_one(d):
            def slot(k, placed):
                group = table[d, k]
                seen = lax.fori_loop(0, k, lambda j, s: jnp.where(table[d, j] == group, 1, s), jnp.int32(0))

                @pl.when(seen == 0)
                def _():
                    to_device(d, group, placed, 1).start()

                return placed + 1 - seen

            placed = lax.fori_loop(0, slots, slot, jnp.int32(0))

            def fill(j, carry):
                to_device(d, table[d, 0], j, 1).start()
                return carry

            lax.fori_loop(placed, span, fill, 0)

        def send(d, carry):
            @pl.when(starts[d] >= 0)
            def _():
                to_device(d, starts[d], 0, span).start()

            @pl.when(starts[d] < 0)
            def _():
                one_by_one(d)

            return carry

        lax.fori_loop(0, devices, send, 0)

    for d in range(devices):
        to_device(d, 0, 0, span).wait()


def pack(blocks_of, slopes, pieces=1):
    steps, samp_dev, width = slopes.shape
    devices, slots = blocks_of.shape
    tall = steps * samp_dev
    window = DISTINCT * BLOCK
    return pl.pallas_call(
        functools.partial(pack_kernel, pieces),
        out_shape=pltpu.HBM((devices, tall, window), slopes.dtype),
        in_specs=[pl.BlockSpec(memory_space=pltpu.HBM)] * 2,
        out_specs=pl.BlockSpec(memory_space=pltpu.HBM),
        scratch_shapes=[
            pltpu.VMEM((devices, slots), jnp.int32),
            pltpu.VMEM((tall, width + window), slopes.dtype),
            pltpu.SMEM((devices,), jnp.int32),
            pltpu.SMEM((devices, slots), jnp.int32),
            pltpu.SemaphoreType.DMA((devices,)),
            pltpu.SemaphoreType.DMA((pieces + 1, steps)),
            pltpu.SemaphoreType.DMA((2,)),
        ],
        compiler_params=pltpu.CompilerParams(vmem_limit_bytes=16 * MIB),
        name="pack_windows",
    )(pltpu.with_memory_space_constraint(blocks_of, pltpu.HBM), pltpu.with_memory_space_constraint(slopes, pltpu.HBM))


def plan_kernel(
    groups, blocks, slope_tab, act_tab, count_tab, weights,
    holder_out, kept,
    slopes, acts, counts, places, holder, table_sems, kept_sems, holder_sem,
):
    slots = weights.shape[0]
    loads = [
        pltpu.make_async_copy(source, held, table_sems.at[i])
        for i, (source, held) in enumerate(((slope_tab, slopes), (act_tab, acts), (count_tab, counts)))
    ]
    for load in loads:
        load.start()
    for load in loads:
        load.wait()
    own = lax.axis_index("samp")
    count = counts[0, own]
    half = groups // 2

    def turn(group):
        return jnp.where(group >= groups - half, group - (groups - half), group + half)

    def extent(k, spans):
        low_end, high_end, low_turned, high_turned = spans
        group = slopes[own, k]
        turned = turn(group)
        return (
            jnp.minimum(low_end, group), jnp.maximum(high_end, group),
            jnp.minimum(low_turned, turned), jnp.maximum(high_turned, turned),
        )

    first = slopes[own, 0]
    low_end, high_end, low_turned, high_turned = lax.fori_loop(
        1, slots, extent, (first, first, turn(first), turn(first))
    )
    straight = high_end - low_end < DISTINCT
    around = high_turned - low_turned < DISTINCT

    def clear(j, carry):
        holder[0, j] = jnp.int32(-1)
        return carry

    lax.fori_loop(0, holder.shape[1], clear, 0)

    def rank(k, placed):
        group = slopes[own, k]
        found = lax.fori_loop(0, k, lambda j, at: jnp.where(slopes[own, j] == group, places[j], at), jnp.int32(-1))
        places[k] = jnp.where(found >= 0, found, placed)
        return jnp.where(found >= 0, placed, placed + 1)

    @pl.when(jnp.logical_not(jnp.logical_or(straight, around)))
    def _():
        lax.fori_loop(0, slots, rank, jnp.int32(0))

    @pl.when(jnp.logical_or(straight, around))
    def _():
        def offset(k, carry):
            group = slopes[own, k]
            places[k] = jnp.where(straight, group - low_end, turn(group) - low_turned)
            return carry

        lax.fori_loop(0, slots, offset, 0)

    def keep(k):
        return pltpu.make_async_copy(weights.at[k], kept.at[k], kept_sems.at[k])

    def start_keep(k, carry):
        keep(k).start()
        return carry

    def wait_keep(k, carry):
        keep(k).wait()
        return carry

    lax.fori_loop(count, slots, start_keep, 0)

    def lay(k, carry):
        holder[0, places[k] * blocks + acts[own, k]] = k
        return carry

    lax.fori_loop(0, count, lay, 0)
    store = pltpu.make_async_copy(holder, holder_out, holder_sem)
    store.start()
    store.wait()
    lax.fori_loop(count, slots, wait_keep, 0)


def plan(groups, blocks, slope_tab, act_tab, count_tab, weights):
    slots = weights.shape[0]
    vmem = pl.BlockSpec(memory_space=pltpu.VMEM)
    hbm = pl.BlockSpec(memory_space=pltpu.HBM)
    return pl.pallas_call(
        functools.partial(plan_kernel, groups, blocks),
        out_shape=[pltpu.VMEM((1, BLOCK), jnp.int32), pltpu.HBM(weights.shape, jnp.float32)],
        in_specs=[hbm, hbm, hbm, vmem],
        out_specs=[vmem, hbm],
        scratch_shapes=[
            pltpu.SMEM(slope_tab.shape, jnp.int32),
            pltpu.SMEM(act_tab.shape, jnp.int32),
            pltpu.SMEM(count_tab.shape, jnp.int32),
            pltpu.SMEM((slots,), jnp.int32),
            pltpu.SMEM((1, BLOCK), jnp.int32),
            pltpu.SemaphoreType.DMA((3,)),
            pltpu.SemaphoreType.DMA((slots,)),
            pltpu.SemaphoreType.DMA,
        ],
        compiler_params=pltpu.CompilerParams(vmem_limit_bytes=16 * MIB),
        cost_estimate=pl.CostEstimate(flops=10**6, bytes_accessed=4 * 10**6, transcendentals=0),
        name="plan_cells",
    )(
        pltpu.with_memory_space_constraint(slope_tab, pltpu.HBM),
        pltpu.with_memory_space_constraint(act_tab, pltpu.HBM),
        pltpu.with_memory_space_constraint(count_tab, pltpu.HBM),
        weights,
    )


def spreader(samples, wide, samp_dev, step, dtype):
    tall = wide * samp_dev // samples
    n = lax.broadcasted_iota(jnp.int32, (samples, wide), 0)
    c = lax.broadcasted_iota(jnp.int32, (samples, wide), 1)
    column = (n // samp_dev) * tall + step * samp_dev + n % samp_dev
    return (c == column).astype(jnp.float32).astype(dtype)


def fit_kernel(
    step_rate, samp_dev, holder, seen, weights, targets, kept,
    fitted, residual, seen_turned, stack, low, rest_low, out_sems, rest_sem,
):
    steps, rows, samples = targets.shape
    count, block, _ = stack.shape
    wide, window = seen.shape
    span = window // block
    blocks = rows // block
    tall = wide * samp_dev // samples
    chunk = 2
    edges = list(range(0, span, chunk)) + [span]
    slot_of = [holder[0, j] for j in range(count)]

    def at_rows(a):
        return slice(a * block, (a + 1) * block)

    def at_cols(p):
        return slice(p * block, (p + 1) * block)

    def held(p, a):
        slot = slot_of[p * blocks + a]
        return jnp.where(slot >= 0, weights[jnp.maximum(slot, 0)], 0.0)

    def put(j, slot):
        return pltpu.make_async_copy(stack.at[j], fitted.at[slot], out_sems.at[j])

    for first, last in zip(edges, edges[1:]):
        at = slice(first * block, last * block)
        seen_turned[at, :] = seen[:, at].T
        for p in range(first, last):
            for a in range(blocks):
                low[at_rows(a), at_cols(p)] = held(p, a).astype(low.dtype)

    picks = [spreader(samples, wide, samp_dev, t, jnp.bfloat16) for t in range(steps)]
    wanted = [jnp.dot(targets[t], picks[t], preferred_element_type=jnp.float32) for t in range(steps)]
    column = lax.broadcasted_iota(jnp.int32, (block, wide), 1)
    step_of = (column % tall) // samp_dev
    store_rest = pltpu.make_async_copy(rest_low, residual, rest_sem)
    rests = [jnp.zeros((block, wide), jnp.bfloat16)] * blocks
    for t in range(steps):
        for a in range(blocks):
            predicted = jnp.dot(low[at_rows(a), :], seen_turned[...], preferred_element_type=jnp.float32)
            rest = (predicted - wanted[t][at_rows(a)]).astype(jnp.bfloat16)
            rests[a] = jnp.where(step_of == t, rest, rests[a])
        both = jnp.concatenate(rests, axis=0)
        if t == steps - 1:
            rest_low[...] = lax.dot_general(
                both, picks[t], (((1,), (1,)), ((), ())), preferred_element_type=jnp.float32
            ).astype(rest_low.dtype)
            store_rest.start()
        for first, last in zip(edges, edges[1:]):
            gradient = jnp.dot(both, seen[:, first * block : last * block], preferred_element_type=jnp.float32)
            pairs = [(p, a) for p in range(first, last) for a in range(blocks)]
            for p, a in pairs:
                j = p * blocks + a
                new = held(p, a) - step_rate * gradient[at_rows(a), at_cols(p - first)]
                if t < steps - 1:
                    low[at_rows(a), at_cols(p)] = jnp.where(slot_of[j] >= 0, new, 0.0).astype(low.dtype)
                else:
                    stack[j] = new
            if t == steps - 1:
                for p, a in pairs:

                    @pl.when(slot_of[p * blocks + a] >= 0)
                    def _(j=p * blocks + a):
                        put(j, slot_of[j]).start()

    store_rest.wait()
    for j in range(count):

        @pl.when(slot_of[j] >= 0)
        def _(j=j):
            put(j, 0).wait()


def fit(step_rate, samp_dev, holder, seen, weights, targets, kept):
    steps, rows, samples = targets.shape
    slots, block, _ = weights.shape
    wide, window = seen.shape
    count = rows // block * DISTINCT
    vmem = pl.BlockSpec(memory_space=pltpu.VMEM)
    hbm = pl.BlockSpec(memory_space=pltpu.HBM)
    return pl.pallas_call(
        functools.partial(fit_kernel, step_rate, samp_dev),
        out_shape=[
            pltpu.HBM(kept.shape, jnp.float32),
            pltpu.HBM((rows, samples), jnp.bfloat16),
        ],
        in_specs=[vmem, vmem, vmem, vmem, hbm],
        out_specs=[hbm, hbm],
        input_output_aliases={4: 0},
        scratch_shapes=[
            pltpu.VMEM((window, wide), seen.dtype),
            pltpu.VMEM((count, block, block), jnp.float32),
            pltpu.VMEM((rows, window), jnp.bfloat16),
            pltpu.VMEM((rows, samples), jnp.bfloat16),
            pltpu.SemaphoreType.DMA((count,)),
            pltpu.SemaphoreType.DMA,
        ],
        compiler_params=pltpu.CompilerParams(vmem_limit_bytes=24 * MIB),
        name="fit_steps",
    )(pltpu.with_memory_space_constraint(holder, pltpu.VMEM), seen, weights, targets, kept)


def fit_over_groups(step_rate, samp_dev, places, acts, arrived, weights, targets):
    steps, rows, samples = targets.shape
    slots, block, _ = weights.shape
    live = places >= 0
    devices = arrived.shape[0]
    grouped = arrived.reshape(devices, steps, samp_dev, DISTINCT, block)
    slot_slopes = jnp.take(grouped, jnp.maximum(places, 0), axis=3)
    blocks = rows // block
    onehot = ((acts[None, :] == jnp.arange(blocks)[:, None]) & live[None, :]).astype(jnp.float32)
    residual = None
    for t in range(steps):
        now = slot_slopes[:, t].reshape(samples, slots, block)
        partial_sums = jnp.einsum(
            "kil,nkl->kin", weights.astype(jnp.bfloat16), now, preferred_element_type=jnp.float32
        )
        summed = jnp.einsum("jk,kin->jin", onehot, partial_sums, precision=lax.Precision.HIGHEST)
        total = lax.psum(summed, "sens")
        residual = (total - targets[t].reshape(blocks, block, samples)).astype(jnp.bfloat16)
        gradient = jnp.einsum(
            "kin,nkl->kil", jnp.take(residual, acts, axis=0), now, preferred_element_type=jnp.float32
        )
        weights = jnp.where(live[:, None, None], weights - step_rate * gradient, weights)
    return weights, residual.reshape(rows, samples)


def per_device(slopes, targets, reconstructor, foot_act, foot_slope, foot_count):
    block = reconstructor.shape[-1]
    slots = reconstructor.shape[2]
    groups = slopes.shape[2] // block
    samp_dev = slopes.shape[1]
    samples = targets.shape[2]
    devices = foot_slope.shape[1]
    step_rate = slots * block / (samples + 3 * slots * block)
    packed = pack(foot_slope[0], slopes)
    arrived = lax.all_to_all(packed, "samp", split_axis=0, concat_axis=0, tiled=True)
    weights = reconstructor[0, 0]
    if lax.axis_size("sens") > 1:
        own_index = lax.axis_index("samp")

        def own(table):
            return lax.dynamic_index_in_dim(table, own_index, 0, keepdims=False)

        places = own_places(own(foot_slope[0]), own(foot_count[0]), groups)
        fitted, residual = fit_over_groups(
            step_rate, samp_dev, places, own(foot_act[0]), arrived, weights, targets
        )
        return fitted[None, None], residual
    blocks = targets.shape[1] // block
    holder, kept = plan(groups, blocks, foot_slope[0], foot_act[0], foot_count, weights)
    seen = arrived.reshape(devices * STEPS * samp_dev, DISTINCT * block)
    fitted, residual = fit(step_rate, samp_dev, holder, seen, weights, targets, kept)
    return fitted[None, None], residual


def solution(mesh):
    return jax.shard_map(
        per_device,
        mesh=mesh,
        in_specs=(
            P(None, "samp", "sens"),
            P(None, "samp", None),
            P("sens", "samp", None, None, None),
            P("sens", None, None),
            P("sens", None, None),
            P("sens", None),
        ),
        out_specs=(P("sens", "samp", None, None, None), P("samp", None)),
        check_vma=False,
    )
```

time: 48.9 us -> 46.7 us (0.955)
  other arithmetic: 8.59 us -> 0 us
  waiting for transfers between devices: 21.7 us -> 28.1 us
  Pallas kernels: 8.38 us -> 10.4 us
  between operations: 1.96 us -> 0.68 us
  local copies, waits for them, and re-layouts: 0.59 us -> 0.01 us
    all_to_all x1, waiting for transfers between devices: 21.7 us -> 28.1 us  [per_device(): lax.all_to_all(packed, 'samp', split_axis=0, concat_axis=0, tiled=True)]
    pallas_call x0 -> x1, Pallas kernels: none -> 4.05 us  [plan(): pl.pallas_call(functools.partial(plan_kernel, groups, blocks), out_shape=...]
    reduce_min x2 -> x0, other arithmetic: 2.73 us -> none  [the longest x1 1.41 us: own_places(): around = turned - jnp.min(turned)]
    select_n x1 -> x0, other arithmetic: 2.6 us -> none  [per_device(): cell = jnp.where(places >= 0, acts * DISTINCT + places, -1)]
    reduce_max x1 -> x0, other arithmetic: 1.95 us -> none  [own_places(): jnp.max(straight) < DISTINCT]
    pallas_call x1, Pallas kernels: 5.23 us -> 3.69 us  [fit(): pl.pallas_call(functools.partial(fit_kernel, step_rate, samp_dev), out_sh...]
    concatenate x1 -> x0, other arithmetic: 0.72 us -> none  [per_device(): holder = jnp.concatenate([holder, count[None]]).astype(jnp.int32)]
    dynamic_slice x1 -> x0, local copies, waits for them, and re-layouts: 0.58 us -> none  [own(): return lax.dynamic_index_in_dim(table, own_index, 0, keepdims=False)]
  transfers between devices with their start and end apart: 1 -> 1, of which waited for: 1 -> 1; matrix products, arithmetic and copies ran while one was open for 19% -> 0% of each run, Pallas kernels for 0% -> 9%
where the time goes in v3:
time: 46.7 us; the launch traced here: 46.4 us
  waiting for transfers between devices  28.1 us (60%)
  Pallas kernels  10.4 us (22%)
  starting transfers between devices  7.3 us (16%)
  between operations  0.68 us (1%)
    all_to_all x1, waiting for transfers between devices, per_device(): lax.all_to_all(packed, 'samp', split_axis=0, concat_axis=0, tiled=True)  28.1 us
    all_to_all x1, starting transfers between devices, per_device(): lax.all_to_all(packed, 'samp', split_axis=0, concat_axis=0, tiled=True)  7.3 us
    pallas_call x1, Pallas kernels, plan(): pl.pallas_call(functools.partial(plan_kernel, groups, blocks), out_shape=...  4.05 us
    pallas_call x1, Pallas kernels, fit(): pl.pallas_call(functools.partial(fit_kernel, step_rate, samp_dev), out_sh...  3.69 us
    pallas_call x1, Pallas kernels, pack(): pl.pallas_call(functools.partial(pack_kernel, pieces), out_shape=pltpu.HB...  2.65 us
  transfers between devices with their start and end apart: 1, of which 1 were waited for; matrix products, arithmetic and copies ran while one was open for 0% of the time, Pallas kernels for 9%

profile of v3, /device:TPU:0, one launch (start us, length us, event | category | flops | bytes accessed | tf_op | source)
XLA Modules:
  0.0 46.4 jit_solution(7831545606537337404)
XLA Ops:
  0.6 0.0 copy-start
  0.6 2.6 %pack_windows.1 = bf16[32,8,2560]{2,1,0:T(8,128)(2,1)} custom-call(s32[32,32]{1,0:T(8,128)} %bitcast.9, bf16[2,4,37632]{2,1,0:T(4,128)(2,1)} %slopes.1), custom_call_target="tpu_custom_call" | custom-call | tf_op jit(solution)/shard_map/pack_windows/pallas_call | solution.py:131
  3.3 0.0 copy-start.1
  3.3 7.3 %all-to-all-start = ((bf16[32,8,2560]{2,1,0:T(8,128)(2,1)}), bf16[32,8,2560]{2,1,0:T(8,128)(2,1)S(1)}, u32[]{:S(2)}, u32[]{:S(2)}) async-start(bf16[32,8,2560]{2,1,0:T(8,128)(2,1)} %pack_windows.1), calls=%async_computation | async-start | bytes 2621440 | tf_op jit(solution)/shard_map/all_to_all | solution.py:413
  10.6 0.0 copy-done
  10.6 4.0 %plan_cells.1 = (s32[1,128]{1,0:T(1,128)S(1)}, f32[32,128,128]{2,1,0:T(8,128)}) custom-call(s32[32,32]{1,0:T(8,128)} %bitcast.10, s32[32,32]{1,0:T(8,128)} %bitcast.11, s32[1,32]{1,0:T(1,128)} %count_tab.1, f32[32,128,128]{2,1,0:T(8,128)S(1)} %bitcast.5), custom_call_target="tpu_custom_call" | custom-call | flops 1000000 | bytes 4000000 | tf_op jit(solution)/shard_map/plan_cells/pallas_call | solution.py:240
  14.7 28.1 %all-to-all-done = bf16[32,8,2560]{2,1,0:T(8,128)(2,1)S(1)} async-done(((bf16[32,8,2560]{2,1,0:T(8,128)(2,1)}), bf16[32,8,2560]{2,1,0:T(8,128)(2,1)S(1)}, u32[]{:S(2)}, u32[]{:S(2)}) %all-to-all-start) | async-done | bytes 1310752 | tf_op jit(solution)/shard_map/all_to_all | solution.py:413
  42.7 0.0 copy-done.1
  42.7 3.7 %fit_steps.1 = (f32[32,128,128]{2,1,0:T(8,128)}, bf16[256,128]{1,0:T(8,128)(2,1)}) custom-call(s32[1,128]{1,0:T(1,128)S(1)} %get-tuple-element.6.holder, bf16[256,2560]{1,0:T(8,128)(2,1)S(1)} %bitcast.7, f32[32,128,128]{2,1,0:T(8,128)S(1)} %bitcast.6, bf16[2,256,128]{2,1,0:T(8,128)(2,1)S(1)} %copy-done.1, ...), custom_call_target="tpu_custom_call", output_to_operand_aliasing={{0}: (4, {})} | custom-call | tf_op jit(solution)/shard_map/fit_steps/pallas_call | solution.py:357
Async XLA Ops:
  0.6 10.0 %copy-start = (f32[1,1,32,128,128]{4,3,2,1,0:T(8,128)S(1)}, f32[1,1,32,128,128]{4,3,2,1,0:T(8,128)}, u32[]{:S(2)}) copy-start(f32[1,1,32,128,128]{4,3,2,1,0:T(8,128)} %param.8) | copy-start | bytes 6291460
  3.3 39.5 %copy-start.1 = (bf16[2,256,128]{2,1,0:T(8,128)(2,1)S(1)}, bf16[2,256,128]{2,1,0:T(8,128)(2,1)}, u32[]{:S(2)}) copy-start(bf16[2,256,128]{2,1,0:T(8,128)(2,1)} %targets.1) | copy-start | bytes 393220
  3.3 39.4 %all-to-all-start = ((bf16[32,8,2560]{2,1,0:T(8,128)(2,1)}), bf16[32,8,2560]{2,1,0:T(8,128)(2,1)S(1)}, u32[]{:S(2)}, u32[]{:S(2)}) async-start(bf16[32,8,2560]{2,1,0:T(8,128)(2,1)} %pack_windows.1), calls=%async_computation | async-start | bytes 2621440 | tf_op jit(solution)/shard_map/all_to_all | solution.py:413

commit v4 on v3

--- a/solution.py
+++ b/solution.py
@@ -263,99 +263,120 @@
     )
 
 
-def spreader(samples, wide, samp_dev, step, dtype):
-    tall = wide * samp_dev // samples
-    n = lax.broadcasted_iota(jnp.int32, (samples, wide), 0)
-    c = lax.broadcasted_iota(jnp.int32, (samples, wide), 1)
-    column = (n // samp_dev) * tall + step * samp_dev + n % samp_dev
-    return (c == column).astype(jnp.float32).astype(dtype)
+def mixer(shape, samples, samp_dev, order, dtype):
+    steps = shape[0] // samples
+    tall = steps * samp_dev
+    line = lax.broadcasted_iota(jnp.int32, (1, shape[1]), 1)
+    turn, inner = line // tall, line % tall
+    source = turn
+    if order != tuple(range(len(order))):
+        source = functools.reduce(jnp.add, [jnp.where(turn == r, d, 0) for r, d in enumerate(order)])
+    row = (inner // samp_dev) * samples + source * samp_dev + inner % samp_dev
+    return (lax.broadcasted_iota(jnp.int32, shape, 0) == row).astype(jnp.float32).astype(dtype), inner // samp_dev
 
 
 def fit_kernel(
-    step_rate, samp_dev, holder, seen, weights, targets, kept,
-    fitted, residual, seen_turned, stack, low, rest_low, out_sems, rest_sem,
+    step_rate, samp_dev, order, holder, seen, weights, targets, kept,
+    fitted, residual, stack, rest_low, out_sems, rest_sem, *sums,
 ):
     steps, rows, samples = targets.shape
     count, block, _ = stack.shape
     wide, window = seen.shape
-    span = window // block
     blocks = rows // block
-    tall = wide * samp_dev // samples
-    chunk = 2
-    edges = list(range(0, span, chunk)) + [span]
+    pair = wide // block
+    tiles = window // wide
     slot_of = [holder[0, j] for j in range(count)]
 
-    def at_rows(a):
-        return slice(a * block, (a + 1) * block)
-
-    def at_cols(p):
-        return slice(p * block, (p + 1) * block)
-
-    def held(p, a):
-        slot = slot_of[p * blocks + a]
+    def region(tile, part):
+        return sums[part * 2 + tile % 2]
+
+    def cell(tile, q, a):
+        return (tile * pair + q) * blocks + a
+
+    def held(j):
+        slot = slot_of[j]
         return jnp.where(slot >= 0, weights[jnp.maximum(slot, 0)], 0.0)
 
-    def put(j, slot):
-        return pltpu.make_async_copy(stack.at[j], fitted.at[slot], out_sems.at[j])
-
-    for first, last in zip(edges, edges[1:]):
-        at = slice(first * block, last * block)
-        seen_turned[at, :] = seen[:, at].T
-        for p in range(first, last):
+    def join(parts):
+        return jnp.concatenate([jnp.concatenate(line, axis=1) for line in parts], axis=0)
+
+    def multiply(tile, lhs, rhs, part, transpose=False):
+        stage = (tile // 2) % 2
+        pltpu.matmul_push_rhs(rhs, stage, tile % 2, transpose=transpose)
+        pltpu.matmul_acc_lhs(region(tile, part), lhs, load_staged_rhs=stage)
+
+    def tile_of(tile):
+        return seen[:, tile * wide : (tile + 1) * wide]
+
+    mix, step_of = mixer((steps * samples, wide), samples, samp_dev, order, jnp.bfloat16)
+    for tile in range(tiles):
+        start = join([[held(cell(tile, q, a)) for q in range(pair)] for a in range(blocks)]).astype(jnp.bfloat16)
+        multiply(tile, start, tile_of(tile), 0, transpose=True)
+    multiply(0, jnp.concatenate([targets[t] for t in range(steps)], axis=1), mix, 1)
+    wanted = pltpu.matmul_pop(region(0, 1))
+    store_rest = pltpu.make_async_copy(rest_low, residual, rest_sem)
+    both = jnp.zeros((rows, wide), jnp.bfloat16)
+    for t in range(steps):
+        predicted = pltpu.matmul_pop(region(0, 0)) + pltpu.matmul_pop(region(1, 0))
+        both = jnp.where(step_of == t, (predicted - wanted).astype(jnp.bfloat16), both)
+        if t == steps - 1:
+            multiply(0, both, mix, 0, transpose=True)
+            last = pltpu.matmul_pop(region(0, 0))
+            rest_low[...] = last[:, t * samples : (t + 1) * samples].astype(rest_low.dtype)
+            store_rest.start()
+        multiply(0, both, tile_of(0), 1)
+        multiply(1, both, tile_of(1), 1)
+        for tile in range(tiles):
+            gradient = pltpu.matmul_pop(region(tile, 1 + (tile // 2) % 2))
+            if tile + 2 < tiles:
+                multiply(tile + 2, both, tile_of(tile + 2), 1 + (tile // 2 + 1) % 2)
+            parts = []
             for a in range(blocks):
-                low[at_rows(a), at_cols(p)] = held(p, a).astype(low.dtype)
-
-    picks = [spreader(samples, wide, samp_dev, t, jnp.bfloat16) for t in range(steps)]
-    wanted = [jnp.dot(targets[t], picks[t], preferred_element_type=jnp.float32) for t in range(steps)]
-    column = lax.broadcasted_iota(jnp.int32, (block, wide), 1)
-    step_of = (column % tall) // samp_dev
-    store_rest = pltpu.make_async_copy(rest_low, residual, rest_sem)
-    rests = [jnp.zeros((block, wide), jnp.bfloat16)] * blocks
-    for t in range(steps):
-        for a in range(blocks):
-            predicted = jnp.dot(low[at_rows(a), :], seen_turned[...], preferred_element_type=jnp.float32)
-            rest = (predicted - wanted[t][at_rows(a)]).astype(jnp.bfloat16)
-            rests[a] = jnp.where(step_of == t, rest, rests[a])
-        both = jnp.concatenate(rests, axis=0)
-        if t == steps - 1:
-            rest_low[...] = lax.dot_general(
-                both, picks[t], (((1,), (1,)), ((), ())), preferred_element_type=jnp.float32
-            ).astype(rest_low.dtype)
-            store_rest.start()
-        for first, last in zip(edges, edges[1:]):
-            gradient = jnp.dot(both, seen[:, first * block : last * block], preferred_element_type=jnp.float32)
-            pairs = [(p, a) for p in range(first, last) for a in range(blocks)]
-            for p, a in pairs:
-                j = p * blocks + a
-                new = held(p, a) - step_rate * gradient[at_rows(a), at_cols(p - first)]
-                if t < steps - 1:
-                    low[at_rows(a), at_cols(p)] = jnp.where(slot_of[j] >= 0, new, 0.0).astype(low.dtype)
-                else:
-                    stack[j] = new
-            if t == steps - 1:
-                for p, a in pairs:
-
-                    @pl.when(slot_of[p * blocks + a] >= 0)
-                    def _(j=p * blocks + a):
-                        put(j, slot_of[j]).start()
+                line = []
+                for q in range(pair):
+                    j = cell(tile, q, a)
+                    moved = gradient[a * block : (a + 1) * block, q * block : (q + 1) * block]
+                    new = held(j) - step_rate * moved
+                    if t < steps - 1:
+                        line.append(jnp.where(slot_of[j] >= 0, new, 0.0))
+                    else:
+                        stack[j] = new
+                parts.append(line)
+            if t < steps - 1:
+                multiply(tile, join(parts).astype(jnp.bfloat16), tile_of(tile), 0, transpose=True)
+            else:
+                for a in range(blocks):
+                    for q in range(pair):
+                        j = cell(tile, q, a)
+
+                        @pl.when(slot_of[j] >= 0)
+                        def _(j=j):
+                            pltpu.make_async_copy(stack.at[j], fitted.at[slot_of[j]], out_sems.at[j]).start()
 
     store_rest.wait()
     for j in range(count):
 
         @pl.when(slot_of[j] >= 0)
         def _(j=j):
-            put(j, 0).wait()
-
-
-def fit(step_rate, samp_dev, holder, seen, weights, targets, kept):
+            pltpu.make_async_copy(stack.at[j], fitted.at[0], out_sems.at[j]).wait()
+
+
+def fit(step_rate, samp_dev, order, holder, seen, weights, targets, kept):
     steps, rows, samples = targets.shape
     slots, block, _ = weights.shape
     wide, window = seen.shape
     count = rows // block * DISTINCT
     vmem = pl.BlockSpec(memory_space=pltpu.VMEM)
     hbm = pl.BlockSpec(memory_space=pltpu.HBM)
+
+    def kernel(*refs):
+        pl.run_scoped(
+            functools.partial(fit_kernel, step_rate, samp_dev, order, *refs),
+            *[pltpu.ACC(unit)((rows, wide), jnp.float32) for part in range(3) for unit in range(2)],
+        )
+
     return pl.pallas_call(
-        functools.partial(fit_kernel, step_rate, samp_dev),
+        kernel,
         out_shape=[
             pltpu.HBM(kept.shape, jnp.float32),
             pltpu.HBM((rows, samples), jnp.bfloat16),
@@ -364,9 +385,7 @@
         out_specs=[hbm, hbm],
         input_output_aliases={4: 0},
         scratch_shapes=[
-            pltpu.VMEM((window, wide), seen.dtype),
             pltpu.VMEM((count, block, block), jnp.float32),
-            pltpu.VMEM((rows, window), jnp.bfloat16),
             pltpu.VMEM((rows, samples), jnp.bfloat16),
             pltpu.SemaphoreType.DMA((count,)),
             pltpu.SemaphoreType.DMA,
@@ -409,6 +428,7 @@
     samples = targets.shape[2]
     devices = foot_slope.shape[1]
     step_rate = slots * block / (samples + 3 * slots * block)
+    order = tuple(range(devices))
     packed = pack(foot_slope[0], slopes)
     arrived = lax.all_to_all(packed, "samp", split_axis=0, concat_axis=0, tiled=True)
     weights = reconstructor[0, 0]
@@ -426,7 +446,7 @@
     blocks = targets.shape[1] // block
     holder, kept = plan(groups, blocks, foot_slope[0], foot_act[0], foot_count, weights)
     seen = arrived.reshape(devices * STEPS * samp_dev, DISTINCT * block)
-    fitted, residual = fit(step_rate, samp_dev, holder, seen, weights, targets, kept)
+    fitted, residual = fit(step_rate, samp_dev, order, holder, seen, weights, targets, kept)
     return fitted[None, None], residual
 
 

time: 46.7 us -> 46.4 us (level)
  Pallas kernels: 10.4 us -> 9.93 us
where the time goes in v4:
time: 46.4 us; the launch traced here: 46 us
  waiting for transfers between devices  28.1 us (61%)
  Pallas kernels  9.93 us (21%)
  starting transfers between devices  7.3 us (16%)
  between operations  0.68 us (1%)
    all_to_all x1, waiting for transfers between devices, per_device(): lax.all_to_all(packed, 'samp', split_axis=0, concat_axis=0, tiled=True)  28.1 us
    all_to_all x1, starting transfers between devices, per_device(): lax.all_to_all(packed, 'samp', split_axis=0, concat_axis=0, tiled=True)  7.3 us
    pallas_call x1, Pallas kernels, plan(): pl.pallas_call(functools.partial(plan_kernel, groups, blocks), out_shape=...  4.05 us
    pallas_call x1, Pallas kernels, fit(): pl.pallas_call(kernel, out_shape=[pltpu.HBM(kept.shape, jnp.float32), plt...  3.24 us
    pallas_call x1, Pallas kernels, pack(): pl.pallas_call(functools.partial(pack_kernel, pieces), out_shape=pltpu.HB...  2.65 us
  transfers between devices with their start and end apart: 1, of which 1 were waited for; matrix products, arithmetic and copies ran while one was open for 0% of the time, Pallas kernels for 9%

profile of v4, /device:TPU:0, one launch (start us, length us, event | category | flops | bytes accessed | tf_op | source)
XLA Modules:
  0.0 46.0 jit_solution(8877812824642293321)
XLA Ops:
  0.6 0.0 copy-start
  0.6 2.6 %pack_windows.1 = bf16[32,8,2560]{2,1,0:T(8,128)(2,1)} custom-call(s32[32,32]{1,0:T(8,128)} %bitcast.9, bf16[2,4,37632]{2,1,0:T(4,128)(2,1)} %slopes.1), custom_call_target="tpu_custom_call" | custom-call | tf_op jit(solution)/shard_map/pack_windows/pallas_call | solution.py:131
  3.3 0.0 copy-start.1
  3.3 7.3 %all-to-all-start = ((bf16[32,8,2560]{2,1,0:T(8,128)(2,1)}), bf16[32,8,2560]{2,1,0:T(8,128)(2,1)S(1)}, u32[]{:S(2)}, u32[]{:S(2)}) async-start(bf16[32,8,2560]{2,1,0:T(8,128)(2,1)} %pack_windows.1), calls=%async_computation | async-start | bytes 2621440 | tf_op jit(solution)/shard_map/all_to_all | solution.py:433
  10.6 0.0 copy-done
  10.6 4.0 %plan_cells.1 = (s32[1,128]{1,0:T(1,128)S(1)}, f32[32,128,128]{2,1,0:T(8,128)}) custom-call(s32[32,32]{1,0:T(8,128)} %bitcast.10, s32[32,32]{1,0:T(8,128)} %bitcast.11, s32[1,32]{1,0:T(1,128)} %count_tab.1, f32[32,128,128]{2,1,0:T(8,128)S(1)} %bitcast.5), custom_call_target="tpu_custom_call" | custom-call | flops 1000000 | bytes 4000000 | tf_op jit(solution)/shard_map/plan_cells/pallas_call | solution.py:240
  14.7 28.1 %all-to-all-done = bf16[32,8,2560]{2,1,0:T(8,128)(2,1)S(1)} async-done(((bf16[32,8,2560]{2,1,0:T(8,128)(2,1)}), bf16[32,8,2560]{2,1,0:T(8,128)(2,1)S(1)}, u32[]{:S(2)}, u32[]{:S(2)}) %all-to-all-start) | async-done | bytes 1310752 | tf_op jit(solution)/shard_map/all_to_all | solution.py:433
  42.7 0.0 copy-done.1
  42.7 3.2 %fit_steps.1 = (f32[32,128,128]{2,1,0:T(8,128)}, bf16[256,128]{1,0:T(8,128)(2,1)}) custom-call(s32[1,128]{1,0:T(1,128)S(1)} %get-tuple-element.6.refs_0_, bf16[256,2560]{1,0:T(8,128)(2,1)S(1)} %bitcast.7, f32[32,128,128]{2,1,0:T(8,128)S(1)} %bitcast.6, bf16[2,256,128]{2,1,0:T(8,128)(2,1)S(1)} %copy-done.1, ...), custom_call_target="tpu_custom_call", output_to_operand_aliasing={{0}: (4, {})} | custom-call | tf_op jit(solution)/shard_map/fit_steps/pallas_call | solution.py:378
Async XLA Ops:
  0.6 10.0 %copy-start = (f32[1,1,32,128,128]{4,3,2,1,0:T(8,128)S(1)}, f32[1,1,32,128,128]{4,3,2,1,0:T(8,128)}, u32[]{:S(2)}) copy-start(f32[1,1,32,128,128]{4,3,2,1,0:T(8,128)} %param.8) | copy-start | bytes 6291460
  3.3 39.5 %copy-start.1 = (bf16[2,256,128]{2,1,0:T(8,128)(2,1)S(1)}, bf16[2,256,128]{2,1,0:T(8,128)(2,1)}, u32[]{:S(2)}) copy-start(bf16[2,256,128]{2,1,0:T(8,128)(2,1)} %refs_3_.1) | copy-start | bytes 393220
  3.3 39.4 %all-to-all-start = ((bf16[32,8,2560]{2,1,0:T(8,128)(2,1)}), bf16[32,8,2560]{2,1,0:T(8,128)(2,1)S(1)}, u32[]{:S(2)}, u32[]{:S(2)}) async-start(bf16[32,8,2560]{2,1,0:T(8,128)(2,1)} %pack_windows.1), calls=%async_computation | async-start | bytes 2621440 | tf_op jit(solution)/shard_map/all_to_all | solution.py:433

commit v5 on v4

--- a/solution.py
+++ b/solution.py
@@ -10,6 +10,9 @@
 STEPS = 2
 DISTINCT = 20
 BLOCK = 128
+ORDERS = {
+    32: (24, 7, 25, 12, 31, 29, 3, 19, 21, 4, 18, 10, 28, 20, 5, 23, 16, 9, 14, 13, 11, 27, 6, 2, 22, 1, 15, 26, 8, 17, 0, 30),
+}
 MIB = 1 << 20
 
 
@@ -30,7 +33,9 @@
     return jnp.where(ids < count_own, place, -1).astype(jnp.int32)
 
 
-def pack_kernel(pieces, blocks_hbm, slopes, out, blocks_of, rows, starts, table, sems, load_sems, table_sems):
+def pack_kernel(
+    pieces, order, blocks_hbm, slopes, out, blocks_of, rows, starts, turns, table, sems, load_sems, table_sems
+):
     steps, samp_dev, width = slopes.shape
     groups = width // BLOCK
     devices, _, window = out.shape
@@ -67,75 +72,79 @@
     for load in loads:
         load.wait()
 
-    def to_device(d, group, at, count):
+    def to_turn(r, group, at, count):
         return pltpu.make_async_copy(
             rows.at[:, pl.ds(pl.multiple_of(group * BLOCK, BLOCK), count * BLOCK)],
-            out.at[d, :, pl.ds(pl.multiple_of(at * BLOCK, BLOCK), count * BLOCK)],
-            sems.at[d],
+            out.at[r, :, pl.ds(pl.multiple_of(at * BLOCK, BLOCK), count * BLOCK)],
+            sems.at[r],
         )
 
     @pl.when(least >= 0)
     def _():
-        for d in range(devices):
-            to_device(d, first_of[d], 0, span).start()
+        for r, d in enumerate(order):
+            to_turn(r, first_of[d], 0, span).start()
 
     @pl.when(least < 0)
     def _():
-        for d in range(devices):
-            starts[d] = first_of[d]
+        for r, d in enumerate(order):
+            starts[r] = first_of[d]
+            turns[r] = jnp.int32(d)
         copy_table = pltpu.make_async_copy(blocks_of, table, table_sems.at[1])
         copy_table.start()
         copy_table.wait()
 
-        def one_by_one(d):
+        def one_by_one(r):
+            d = turns[r]
+
             def slot(k, placed):
                 group = table[d, k]
                 seen = lax.fori_loop(0, k, lambda j, s: jnp.where(table[d, j] == group, 1, s), jnp.int32(0))
 
                 @pl.when(seen == 0)
                 def _():
-                    to_device(d, group, placed, 1).start()
+                    to_turn(r, group, placed, 1).start()
 
                 return placed + 1 - seen
 
             placed = lax.fori_loop(0, slots, slot, jnp.int32(0))
 
             def fill(j, carry):
-                to_device(d, table[d, 0], j, 1).start()
+                to_turn(r, table[d, 0], j, 1).start()
                 return carry
 
             lax.fori_loop(placed, span, fill, 0)
 
-        def send(d, carry):
-            @pl.when(starts[d] >= 0)
+        def send(r, carry):
+            @pl.when(starts[r] >= 0)
             def _():
-                to_device(d, starts[d], 0, span).start()
-
-            @pl.when(starts[d] < 0)
+                to_turn(r, starts[r], 0, span).start()
+
+            @pl.when(starts[r] < 0)
             def _():
-                one_by_one(d)
+                one_by_one(r)
 
             return carry
 
         lax.fori_loop(0, devices, send, 0)
 
-    for d in range(devices):
-        to_device(d, 0, 0, span).wait()
-
-
-def pack(blocks_of, slopes, pieces=1):
+    for r in range(devices):
+        to_turn(r, 0, 0, span).wait()
+
+
+def pack(order, blocks_of, slopes, pieces=1):
     steps, samp_dev, width = slopes.shape
     devices, slots = blocks_of.shape
     tall = steps * samp_dev
     window = DISTINCT * BLOCK
     return pl.pallas_call(
-        functools.partial(pack_kernel, pieces),
+        functools.partial(pack_kernel, pieces, order),
         out_shape=pltpu.HBM((devices, tall, window), slopes.dtype),
         in_specs=[pl.BlockSpec(memory_space=pltpu.HBM)] * 2,
         out_specs=pl.BlockSpec(memory_space=pltpu.HBM),
         scratch_shapes=[
             pltpu.VMEM((devices, slots), jnp.int32),
             pltpu.VMEM((tall, width + window), slopes.dtype),
+            pltpu.SMEM((devices,), jnp.int32),
             pltpu.SMEM((devices,), jnp.int32),
             pltpu.SMEM((devices, slots), jnp.int32),
             pltpu.SemaphoreType.DMA((devices,)),
@@ -395,11 +404,13 @@
     )(pltpu.with_memory_space_constraint(holder, pltpu.VMEM), seen, weights, targets, kept)
 
 
-def fit_over_groups(step_rate, samp_dev, places, acts, arrived, weights, targets):
+def fit_over_groups(step_rate, samp_dev, order, places, acts, arrived, weights, targets):
     steps, rows, samples = targets.shape
     slots, block, _ = weights.shape
     live = places >= 0
     devices = arrived.shape[0]
+    if order != tuple(range(devices)):
+        arrived = jnp.stack([arrived[order.index(d)] for d in range(devices)])
     grouped = arrived.reshape(devices, steps, samp_dev, DISTINCT, block)
     slot_slopes = jnp.take(grouped, jnp.maximum(places, 0), axis=3)
     blocks = rows // block
@@ -428,11 +439,13 @@
     samples = targets.shape[2]
     devices = foot_slope.shape[1]
     step_rate = slots * block / (samples + 3 * slots * block)
-    order = tuple(range(devices))
-    packed = pack(foot_slope[0], slopes)
-    arrived = lax.all_to_all(packed, "samp", split_axis=0, concat_axis=0, tiled=True)
+    order = ORDERS.get(devices, tuple(range(devices)))
+    packed = pack(order, foot_slope[0], slopes)
+    arrived = lax.all_to_all(
+        packed, "samp", split_axis=0, concat_axis=0, tiled=True, axis_index_groups=[list(order)]
+    )
     weights = reconstructor[0, 0]
-    if lax.axis_size("sens") > 1:
+    if lax.axis_size("sens") > 1 or devices * STEPS * samp_dev != 2 * block or targets.shape[1] != 2 * block:
         own_index = lax.axis_index("samp")
 
         def own(table):
@@ -440,7 +453,7 @@
 
         places = own_places(own(foot_slope[0]), own(foot_count[0]), groups)
         fitted, residual = fit_over_groups(
-            step_rate, samp_dev, places, own(foot_act[0]), arrived, weights, targets
+            step_rate, samp_dev, order, places, own(foot_act[0]), arrived, weights, targets
         )
         return fitted[None, None], residual
     blocks = targets.shape[1] // block

time: 46.4 us -> 45.1 us (0.972)
  the two profiles are of different devices: /device:TPU:0 before, /device:TPU:2 now
where the time goes in v5:
time: 45.1 us; the launch traced here: 44.8 us
  waiting for transfers between devices  28 us (62%)
  Pallas kernels  9.99 us (22%)
  starting transfers between devices  6.13 us (14%)
  between operations  0.68 us (2%)
    all_to_all x1, waiting for transfers between devices, per_device(): lax.all_to_all(packed, 'samp', split_axis=0, concat_axis=0, tiled=True, a...  28 us
    all_to_all x1, starting transfers between devices, per_device(): lax.all_to_all(packed, 'samp', split_axis=0, concat_axis=0, tiled=True, a...  6.13 us
    pallas_call x1, Pallas kernels, plan(): pl.pallas_call(functools.partial(plan_kernel, groups, blocks), out_shape=...  4.03 us
    pallas_call x1, Pallas kernels, fit(): pl.pallas_call(kernel, out_shape=[pltpu.HBM(kept.shape, jnp.float32), plt...  3.31 us
    pallas_call x1, Pallas kernels, pack(): pl.pallas_call(functools.partial(pack_kernel, pieces, order), out_shape=p...  2.65 us
  transfers between devices with their start and end apart: 1, of which 1 were waited for; matrix products, arithmetic and copies ran while one was open for 0% of the time, Pallas kernels for 9%

profile of v5, /device:TPU:2, one launch (start us, length us, event | category | flops | bytes accessed | tf_op | source)
XLA Modules:
  0.0 44.8 jit_solution(17184316665632591491)
XLA Ops:
  0.6 0.0 copy-start
  0.6 2.6 %pack_windows.1 = bf16[32,8,2560]{2,1,0:T(8,128)(2,1)} custom-call(s32[32,32]{1,0:T(8,128)} %bitcast.9, bf16[2,4,37632]{2,1,0:T(4,128)(2,1)} %slopes.1), custom_call_target="tpu_custom_call" | custom-call | tf_op jit(solution)/shard_map/pack_windows/pallas_call | solution.py:139
  3.3 0.0 copy-start.1
  3.3 6.1 %all-to-all-start = ((bf16[32,8,2560]{2,1,0:T(8,128)(2,1)}), bf16[32,8,2560]{2,1,0:T(8,128)(2,1)S(1)}, u32[]{:S(2)}, u32[]{:S(2)}) async-start(bf16[32,8,2560]{2,1,0:T(8,128)(2,1)} %pack_windows.1), calls=%async_computation | async-start | bytes 2621440 | tf_op jit(solution)/shard_map/all_to_all | solution.py:444
  9.4 0.0 copy-done
  9.5 4.0 %plan_cells.1 = (s32[1,128]{1,0:T(1,128)S(1)}, f32[32,128,128]{2,1,0:T(8,128)}) custom-call(s32[32,32]{1,0:T(8,128)} %bitcast.10, s32[32,32]{1,0:T(8,128)} %bitcast.11, s32[1,32]{1,0:T(1,128)} %count_tab.1, f32[32,128,128]{2,1,0:T(8,128)S(1)} %bitcast.5), custom_call_target="tpu_custom_call" | custom-call | flops 1000000 | bytes 4000000 | tf_op jit(solution)/shard_map/plan_cells/pallas_call | solution.py:249
  13.5 28.0 %all-to-all-done = bf16[32,8,2560]{2,1,0:T(8,128)(2,1)S(1)} async-done(((bf16[32,8,2560]{2,1,0:T(8,128)(2,1)}), bf16[32,8,2560]{2,1,0:T(8,128)(2,1)S(1)}, u32[]{:S(2)}, u32[]{:S(2)}) %all-to-all-start) | async-done | bytes 1310752 | tf_op jit(solution)/shard_map/all_to_all | solution.py:444
  41.5 0.0 copy-done.1
  41.5 3.3 %fit_steps.1 = (f32[32,128,128]{2,1,0:T(8,128)}, bf16[256,128]{1,0:T(8,128)(2,1)}) custom-call(s32[1,128]{1,0:T(1,128)S(1)} %get-tuple-element.6.refs_0_, bf16[256,2560]{1,0:T(8,128)(2,1)S(1)} %bitcast.7, f32[32,128,128]{2,1,0:T(8,128)S(1)} %bitcast.6, bf16[2,256,128]{2,1,0:T(8,128)(2,1)S(1)} %copy-done.1, ...), custom_call_target="tpu_custom_call", output_to_operand_aliasing={{0}: (4, {})} | custom-call | tf_op jit(solution)/shard_map/fit_steps/pallas_call | solution.py:387
Async XLA Ops:
  0.6 8.8 %copy-start = (f32[1,1,32,128,128]{4,3,2,1,0:T(8,128)S(1)}, f32[1,1,32,128,128]{4,3,2,1,0:T(8,128)}, u32[]{:S(2)}) copy-start(f32[1,1,32,128,128]{4,3,2,1,0:T(8,128)} %param.8) | copy-start | bytes 6291460
  3.3 38.2 %copy-start.1 = (bf16[2,256,128]{2,1,0:T(8,128)(2,1)S(1)}, bf16[2,256,128]{2,1,0:T(8,128)(2,1)}, u32[]{:S(2)}) copy-start(bf16[2,256,128]{2,1,0:T(8,128)(2,1)} %refs_3_.1) | copy-start | bytes 393220
  3.3 38.2 %all-to-all-start = ((bf16[32,8,2560]{2,1,0:T(8,128)(2,1)}), bf16[32,8,2560]{2,1,0:T(8,128)(2,1)S(1)}, u32[]{:S(2)}, u32[]{:S(2)}) async-start(bf16[32,8,2560]{2,1,0:T(8,128)(2,1)} %pack_windows.1), calls=%async_computation | async-start | bytes 2621440 | tf_op jit(solution)/shard_map/all_to_all | solution.py:444

commit v6 on v5

--- a/solution.py
+++ b/solution.py
@@ -11,7 +11,7 @@
 DISTINCT = 20
 BLOCK = 128
 ORDERS = {
-    32: (24, 7, 25, 12, 31, 29, 3, 19, 21, 4, 18, 10, 28, 20, 5, 23, 16, 9, 14, 13, 11, 27, 6, 2, 22, 1, 15, 26, 8, 17, 0, 30),
+    32: (10, 22, 11, 9, 31, 25, 3, 5, 2, 14, 24, 13, 28, 27, 4, 12, 7, 15, 19, 16, 29, 20, 6, 21, 26, 1, 23, 8, 18, 17, 0, 30),
 }
 MIB = 1 << 20
 
@@ -303,8 +303,10 @@
         return (tile * pair + q) * blocks + a
 
     def held(j):
-        slot = slot_of[j]
-        return jnp.where(slot >= 0, weights[jnp.maximum(slot, 0)], 0.0)
+        return weights[jnp.maximum(slot_of[j], 0)]
+
+    def live(j, value):
+        return jnp.where(slot_of[j] >= 0, value, 0.0)
 
     def join(parts):
         return jnp.concatenate([jnp.concatenate(line, axis=1) for line in parts], axis=0)
@@ -318,24 +320,26 @@
         return seen[:, tile * wide : (tile + 1) * wide]
 
     mix, step_of = mixer((steps * samples, wide), samples, samp_dev, order, jnp.bfloat16)
+    multiply(0, jnp.concatenate([targets[t] for t in range(steps)], axis=1), mix, 1)
     for tile in range(tiles):
-        start = join([[held(cell(tile, q, a)) for q in range(pair)] for a in range(blocks)]).astype(jnp.bfloat16)
+        cells = [[cell(tile, q, a) for q in range(pair)] for a in range(blocks)]
+        start = join([[live(j, held(j)) for j in line] for line in cells]).astype(jnp.bfloat16)
         multiply(tile, start, tile_of(tile), 0, transpose=True)
-    multiply(0, jnp.concatenate([targets[t] for t in range(steps)], axis=1), mix, 1)
     wanted = pltpu.matmul_pop(region(0, 1))
     store_rest = pltpu.make_async_copy(rest_low, residual, rest_sem)
     both = jnp.zeros((rows, wide), jnp.bfloat16)
     for t in range(steps):
         predicted = pltpu.matmul_pop(region(0, 0)) + pltpu.matmul_pop(region(1, 0))
         both = jnp.where(step_of == t, (predicted - wanted).astype(jnp.bfloat16), both)
-        if t == steps - 1:
-            multiply(0, both, mix, 0, transpose=True)
-            last = pltpu.matmul_pop(region(0, 0))
-            rest_low[...] = last[:, t * samples : (t + 1) * samples].astype(rest_low.dtype)
-            store_rest.start()
         multiply(0, both, tile_of(0), 1)
         multiply(1, both, tile_of(1), 1)
         for tile in range(tiles):
+            if t == steps - 1 and tile == 1:
+                multiply(0, both, mix, 0, transpose=True)
+            if t == steps - 1 and tile == 3:
+                last = pltpu.matmul_pop(region(0, 0))
+                rest_low[...] = last[:, t * samples : (t + 1) * samples].astype(rest_low.dtype)
+                store_rest.start()
             gradient = pltpu.matmul_pop(region(tile, 1 + (tile // 2) % 2))
             if tile + 2 < tiles:
                 multiply(tile + 2, both, tile_of(tile + 2), 1 + (tile // 2 + 1) % 2)
@@ -347,7 +351,7 @@
                     moved = gradient[a * block : (a + 1) * block, q * block : (q + 1) * block]
                     new = held(j) - step_rate * moved
                     if t < steps - 1:
-                        line.append(jnp.where(slot_of[j] >= 0, new, 0.0))
+                        line.append(live(j, new))
                     else:
                         stack[j] = new
                 parts.append(line)

time: 45.1 us -> 44.1 us (0.978)
  the two profiles are of different devices: /device:TPU:2 before, /device:TPU:1 now
where the time goes in v6:
time: 44.1 us; the launch traced here: 43.9 us
  waiting for transfers between devices  26.1 us (59%)
  Pallas kernels  9.97 us (23%)
  starting transfers between devices  7.1 us (16%)
  between operations  0.68 us (2%)
    all_to_all x1, waiting for transfers between devices, per_device(): lax.all_to_all(packed, 'samp', split_axis=0, concat_axis=0, tiled=True, a...  26.1 us
    all_to_all x1, starting transfers between devices, per_device(): lax.all_to_all(packed, 'samp', split_axis=0, concat_axis=0, tiled=True, a...  7.1 us
    pallas_call x1, Pallas kernels, plan(): pl.pallas_call(functools.partial(plan_kernel, groups, blocks), out_shape=...  4.03 us
    pallas_call x1, Pallas kernels, fit(): pl.pallas_call(kernel, out_shape=[pltpu.HBM(kept.shape, jnp.float32), plt...  3.29 us
    pallas_call x1, Pallas kernels, pack(): pl.pallas_call(functools.partial(pack_kernel, pieces, order), out_shape=p...  2.65 us
  transfers between devices with their start and end apart: 1, of which 1 were waited for; matrix products, arithmetic and copies ran while one was open for 0% of the time, Pallas kernels for 9%

profile of v6, /device:TPU:1, one launch (start us, length us, event | category | flops | bytes accessed | tf_op | source)
XLA Modules:
  0.0 43.9 jit_solution(10210498920119363687)
XLA Ops:
  0.6 0.0 copy-start
  0.6 2.6 %pack_windows.1 = bf16[32,8,2560]{2,1,0:T(8,128)(2,1)} custom-call(s32[32,32]{1,0:T(8,128)} %bitcast.9, bf16[2,4,37632]{2,1,0:T(4,128)(2,1)} %slopes.1), custom_call_target="tpu_custom_call" | custom-call | tf_op jit(solution)/shard_map/pack_windows/pallas_call | solution.py:139
  3.3 0.0 copy-start.1
  3.3 7.1 %all-to-all-start = ((bf16[32,8,2560]{2,1,0:T(8,128)(2,1)}), bf16[32,8,2560]{2,1,0:T(8,128)(2,1)S(1)}, u32[]{:S(2)}, u32[]{:S(2)}) async-start(bf16[32,8,2560]{2,1,0:T(8,128)(2,1)} %pack_windows.1), calls=%async_computation | async-start | bytes 2621440 | tf_op jit(solution)/shard_map/all_to_all | solution.py:448
  10.4 0.0 copy-done
  10.4 4.0 %plan_cells.1 = (s32[1,128]{1,0:T(1,128)S(1)}, f32[32,128,128]{2,1,0:T(8,128)}) custom-call(s32[32,32]{1,0:T(8,128)} %bitcast.10, s32[32,32]{1,0:T(8,128)} %bitcast.11, s32[1,32]{1,0:T(1,128)} %count_tab.1, f32[32,128,128]{2,1,0:T(8,128)S(1)} %bitcast.5), custom_call_target="tpu_custom_call" | custom-call | flops 1000000 | bytes 4000000 | tf_op jit(solution)/shard_map/plan_cells/pallas_call | solution.py:249
  14.5 26.1 %all-to-all-done = bf16[32,8,2560]{2,1,0:T(8,128)(2,1)S(1)} async-done(((bf16[32,8,2560]{2,1,0:T(8,128)(2,1)}), bf16[32,8,2560]{2,1,0:T(8,128)(2,1)S(1)}, u32[]{:S(2)}, u32[]{:S(2)}) %all-to-all-start) | async-done | bytes 1310752 | tf_op jit(solution)/shard_map/all_to_all | solution.py:448
  40.6 0.0 copy-done.1
  40.6 3.3 %fit_steps.1 = (f32[32,128,128]{2,1,0:T(8,128)}, bf16[256,128]{1,0:T(8,128)(2,1)}) custom-call(s32[1,128]{1,0:T(1,128)S(1)} %get-tuple-element.6.refs_0_, bf16[256,2560]{1,0:T(8,128)(2,1)S(1)} %bitcast.7, f32[32,128,128]{2,1,0:T(8,128)S(1)} %bitcast.6, bf16[2,256,128]{2,1,0:T(8,128)(2,1)S(1)} %copy-done.1, ...), custom_call_target="tpu_custom_call", output_to_operand_aliasing={{0}: (4, {})} | custom-call | tf_op jit(solution)/shard_map/fit_steps/pallas_call | solution.py:391
Async XLA Ops:
  0.6 9.8 %copy-start = (f32[1,1,32,128,128]{4,3,2,1,0:T(8,128)S(1)}, f32[1,1,32,128,128]{4,3,2,1,0:T(8,128)}, u32[]{:S(2)}) copy-start(f32[1,1,32,128,128]{4,3,2,1,0:T(8,128)} %param.8) | copy-start | bytes 6291460
  3.3 37.3 %copy-start.1 = (bf16[2,256,128]{2,1,0:T(8,128)(2,1)S(1)}, bf16[2,256,128]{2,1,0:T(8,128)(2,1)}, u32[]{:S(2)}) copy-start(bf16[2,256,128]{2,1,0:T(8,128)(2,1)} %refs_3_.1) | copy-start | bytes 393220
  3.3 37.3 %all-to-all-start = ((bf16[32,8,2560]{2,1,0:T(8,128)(2,1)}), bf16[32,8,2560]{2,1,0:T(8,128)(2,1)S(1)}, u32[]{:S(2)}, u32[]{:S(2)}) async-start(bf16[32,8,2560]{2,1,0:T(8,128)(2,1)} %pack_windows.1), calls=%async_computation | async-start | bytes 2621440 | tf_op jit(solution)/shard_map/all_to_all | solution.py:448

commit v7 on v6

--- a/solution.py
+++ b/solution.py
@@ -157,9 +157,9 @@
 
 
 def plan_kernel(
-    groups, blocks, slope_tab, act_tab, count_tab, weights,
-    holder_out, kept,
-    slopes, acts, counts, places, holder, table_sems, kept_sems, holder_sem,
+    groups, blocks, slope_tab, act_tab, count_tab, weights_hbm,
+    holder_out, kept, weights,
+    slopes, acts, counts, places, holder, table_sems, kept_sems, holder_sem, weights_sem,
 ):
     slots = weights.shape[0]
     loads = [
@@ -168,6 +168,8 @@
     ]
     for load in loads:
         load.start()
+    load_weights = pltpu.make_async_copy(weights_hbm, weights, weights_sem)
+    load_weights.start()
     for load in loads:
         load.wait()
     own = lax.axis_index("samp")
@@ -229,6 +231,7 @@
         keep(k).wait()
         return carry
 
+    load_weights.wait()
     lax.fori_loop(count, slots, start_keep, 0)
 
     def lay(k, carry):
@@ -248,9 +251,13 @@
     hbm = pl.BlockSpec(memory_space=pltpu.HBM)
     return pl.pallas_call(
         functools.partial(plan_kernel, groups, blocks),
-        out_shape=[pltpu.VMEM((1, BLOCK), jnp.int32), pltpu.HBM(weights.shape, jnp.float32)],
-        in_specs=[hbm, hbm, hbm, vmem],
-        out_specs=[vmem, hbm],
+        out_shape=[
+            pltpu.VMEM((1, BLOCK), jnp.int32),
+            pltpu.HBM(weights.shape, jnp.float32),
+            pltpu.VMEM(weights.shape, jnp.float32),
+        ],
+        in_specs=[hbm, hbm, hbm, hbm],
+        out_specs=[vmem, hbm, vmem],
         scratch_shapes=[
             pltpu.SMEM(slope_tab.shape, jnp.int32),
             pltpu.SMEM(act_tab.shape, jnp.int32),
@@ -260,6 +267,7 @@
             pltpu.SemaphoreType.DMA((3,)),
             pltpu.SemaphoreType.DMA((slots,)),
             pltpu.SemaphoreType.DMA,
+            pltpu.SemaphoreType.DMA,
         ],
         compiler_params=pltpu.CompilerParams(vmem_limit_bytes=16 * MIB),
         cost_estimate=pl.CostEstimate(flops=10**6, bytes_accessed=4 * 10**6, transcendentals=0),
@@ -268,7 +276,7 @@
         pltpu.with_memory_space_constraint(slope_tab, pltpu.HBM),
         pltpu.with_memory_space_constraint(act_tab, pltpu.HBM),
         pltpu.with_memory_space_constraint(count_tab, pltpu.HBM),
-        weights,
+        pltpu.with_memory_space_constraint(weights, pltpu.HBM),
     )
 
 
@@ -405,7 +413,13 @@
         ],
         compiler_params=pltpu.CompilerParams(vmem_limit_bytes=24 * MIB),
         name="fit_steps",
-    )(pltpu.with_memory_space_constraint(holder, pltpu.VMEM), seen, weights, targets, kept)
+    )(
+        pltpu.with_memory_space_constraint(holder, pltpu.VMEM),
+        seen,
+        pltpu.with_memory_space_constraint(weights, pltpu.VMEM),
+        targets,
+        kept,
+    )
 
 
 def fit_over_groups(step_rate, samp_dev, order, places, acts, arrived, weights, targets):
@@ -461,7 +475,7 @@
         )
         return fitted[None, None], residual
     blocks = targets.shape[1] // block
-    holder, kept = plan(groups, blocks, foot_slope[0], foot_act[0], foot_count, weights)
+    holder, kept, weights = plan(groups, blocks, foot_slope[0], foot_act[0], foot_count, weights)
     seen = arrived.reshape(devices * STEPS * samp_dev, DISTINCT * block)
     fitted, residual = fit(step_rate, samp_dev, order, holder, seen, weights, targets, kept)
     return fitted[None, None], residual

time: 44.1 us -> 44 us (level)
  no operation moved by 1% of the time
where the time goes in v7:
time: 44 us; the launch traced here: 43.7 us
  waiting for transfers between devices  26.1 us (59%)
  Pallas kernels  9.8 us (22%)
  starting transfers between devices  7.1 us (16%)
  between operations  0.66 us (2%)
    all_to_all x1, waiting for transfers between devices, per_device(): lax.all_to_all(packed, 'samp', split_axis=0, concat_axis=0, tiled=True, a...  26.1 us
    all_to_all x1, starting transfers between devices, per_device(): lax.all_to_all(packed, 'samp', split_axis=0, concat_axis=0, tiled=True, a...  7.1 us
    pallas_call x1, Pallas kernels, plan(): pl.pallas_call(functools.partial(plan_kernel, groups, blocks), out_shape=...  4.04 us
    pallas_call x1, Pallas kernels, fit(): pl.pallas_call(kernel, out_shape=[pltpu.HBM(kept.shape, jnp.float32), plt...  3.26 us
    pallas_call x1, Pallas kernels, pack(): pl.pallas_call(functools.partial(pack_kernel, pieces, order), out_shape=p...  2.5 us
  transfers between devices with their start and end apart: 1, of which 1 were waited for; matrix products, arithmetic and copies ran while one was open for 0% of the time, Pallas kernels for 9%

profile of v7, /device:TPU:1, one launch (start us, length us, event | category | flops | bytes accessed | tf_op | source)
XLA Modules:
  0.0 43.7 jit_solution(14737922678464731066)
XLA Ops:
  0.6 2.5 %pack_windows.1 = bf16[32,8,2560]{2,1,0:T(8,128)(2,1)} custom-call(s32[32,32]{1,0:T(8,128)} %bitcast.8, bf16[2,4,37632]{2,1,0:T(4,128)(2,1)} %slopes.1), custom_call_target="tpu_custom_call" | custom-call | tf_op jit(solution)/shard_map/pack_windows/pallas_call | solution.py:139
  3.1 0.0 copy-start
  3.2 7.1 %all-to-all-start = ((bf16[32,8,2560]{2,1,0:T(8,128)(2,1)}), bf16[32,8,2560]{2,1,0:T(8,128)(2,1)S(1)}, u32[]{:S(2)}, u32[]{:S(2)}) async-start(bf16[32,8,2560]{2,1,0:T(8,128)(2,1)} %pack_windows.1), calls=%async_computation | async-start | bytes 2621440 | tf_op jit(solution)/shard_map/all_to_all | solution.py:462
  10.3 4.0 %plan_cells.1 = (s32[1,128]{1,0:T(1,128)S(1)}, f32[32,128,128]{2,1,0:T(8,128)}, f32[32,128,128]{2,1,0:T(8,128)S(1)}) custom-call(s32[32,32]{1,0:T(8,128)} %bitcast.9, s32[32,32]{1,0:T(8,128)} %bitcast.10, s32[1,32]{1,0:T(1,128)} %count_tab.1, f32[32,128,128]{2,1,0:T(8,128)} %bitcast.7), custom_call_target="tpu_custom_call" | custom-call | flops 1000000 | bytes 4000000 | tf_op jit(solution)/shard_map/plan_cells/pallas_call | solution.py:252
  14.3 26.1 %all-to-all-done = bf16[32,8,2560]{2,1,0:T(8,128)(2,1)S(1)} async-done(((bf16[32,8,2560]{2,1,0:T(8,128)(2,1)}), bf16[32,8,2560]{2,1,0:T(8,128)(2,1)S(1)}, u32[]{:S(2)}, u32[]{:S(2)}) %all-to-all-start) | async-done | bytes 1310752 | tf_op jit(solution)/shard_map/all_to_all | solution.py:462
  40.5 0.0 copy-done
  40.5 3.3 %fit_steps.1 = (f32[32,128,128]{2,1,0:T(8,128)}, bf16[256,128]{1,0:T(8,128)(2,1)}) custom-call(s32[1,128]{1,0:T(1,128)S(1)} %get-tuple-element.7.refs_0_, bf16[256,2560]{1,0:T(8,128)(2,1)S(1)} %bitcast.5, f32[32,128,128]{2,1,0:T(8,128)S(1)} %get-tuple-element.8.refs_2_, bf16[2,256,128]{2,1,0:T(8,128)(2,1)S(1)} %copy-done, ...), custom_call_target="tpu_custom_call", output_to_operand_aliasing={{0}: (4, {})} | custom-call | tf_op jit(solution)/shard_map/fit_steps/pallas_call | solution.py:399
Async XLA Ops:
  3.1 37.3 %copy-start = (bf16[2,256,128]{2,1,0:T(8,128)(2,1)S(1)}, bf16[2,256,128]{2,1,0:T(8,128)(2,1)}, u32[]{:S(2)}) copy-start(bf16[2,256,128]{2,1,0:T(8,128)(2,1)} %refs_3_.1) | copy-start | bytes 393220
  3.2 37.3 %all-to-all-start = ((bf16[32,8,2560]{2,1,0:T(8,128)(2,1)}), bf16[32,8,2560]{2,1,0:T(8,128)(2,1)S(1)}, u32[]{:S(2)}, u32[]{:S(2)}) async-start(bf16[32,8,2560]{2,1,0:T(8,128)(2,1)} %pack_windows.1), calls=%async_computation | async-start | bytes 2621440 | tf_op jit(solution)/shard_map/all_to_all | solution.py:462

commit v8 on v7

--- a/solution.py
+++ b/solution.py
@@ -365,10 +365,9 @@
                 parts.append(line)
             if t < steps - 1:
                 multiply(tile, join(parts).astype(jnp.bfloat16), tile_of(tile), 0, transpose=True)
-            else:
-                for a in range(blocks):
-                    for q in range(pair):
-                        j = cell(tile, q, a)
+            elif tile % 2 == 1 or tile == tiles - 1:
+                for p in range(tile - tile % 2, tile + 1):
+                    for j in range(cell(p, 0, 0), cell(p + 1, 0, 0)):
 
                         @pl.when(slot_of[j] >= 0)
                         def _(j=j):

time: 44 us -> 43.9 us (level)
  the two profiles are of different devices: /device:TPU:1 before, /device:TPU:6 now
where the time goes in v8:
time: 43.9 us; the launch traced here: 43.7 us
  waiting for transfers between devices  27.1 us (62%)
  Pallas kernels  9.77 us (22%)
  starting transfers between devices  6.08 us (14%)
  between operations  0.66 us (2%)
    all_to_all x1, waiting for transfers between devices, per_device(): lax.all_to_all(packed, 'samp', split_axis=0, concat_axis=0, tiled=True, a...  27.1 us
    all_to_all x1, starting transfers between devices, per_device(): lax.all_to_all(packed, 'samp', split_axis=0, concat_axis=0, tiled=True, a...  6.08 us
    pallas_call x1, Pallas kernels, plan(): pl.pallas_call(functools.partial(plan_kernel, groups, blocks), out_shape=...  4.03 us
    pallas_call x1, Pallas kernels, fit(): pl.pallas_call(kernel, out_shape=[pltpu.HBM(kept.shape, jnp.float32), plt...  3.23 us
    pallas_call x1, Pallas kernels, pack(): pl.pallas_call(functools.partial(pack_kernel, pieces, order), out_shape=p...  2.5 us
  transfers between devices with their start and end apart: 1, of which 1 were waited for; matrix products, arithmetic and copies ran while one was open for 0% of the time, Pallas kernels for 9%

profile of v8, /device:TPU:6, one launch (start us, length us, event | category | flops | bytes accessed | tf_op | source)
XLA Modules:
  0.0 43.7 jit_solution(16819095449469498432)
XLA Ops:
  0.6 2.5 %pack_windows.1 = bf16[32,8,2560]{2,1,0:T(8,128)(2,1)} custom-call(s32[32,32]{1,0:T(8,128)} %bitcast.8, bf16[2,4,37632]{2,1,0:T(4,128)(2,1)} %slopes.1), custom_call_target="tpu_custom_call" | custom-call | tf_op jit(solution)/shard_map/pack_windows/pallas_call | solution.py:139
  3.1 0.0 copy-start
  3.2 6.1 %all-to-all-start = ((bf16[32,8,2560]{2,1,0:T(8,128)(2,1)}), bf16[32,8,2560]{2,1,0:T(8,128)(2,1)S(1)}, u32[]{:S(2)}, u32[]{:S(2)}) async-start(bf16[32,8,2560]{2,1,0:T(8,128)(2,1)} %pack_windows.1), calls=%async_computation | async-start | bytes 2621440 | tf_op jit(solution)/shard_map/all_to_all | solution.py:461
  9.2 4.0 %plan_cells.1 = (s32[1,128]{1,0:T(1,128)S(1)}, f32[32,128,128]{2,1,0:T(8,128)}, f32[32,128,128]{2,1,0:T(8,128)S(1)}) custom-call(s32[32,32]{1,0:T(8,128)} %bitcast.9, s32[32,32]{1,0:T(8,128)} %bitcast.10, s32[1,32]{1,0:T(1,128)} %count_tab.1, f32[32,128,128]{2,1,0:T(8,128)} %bitcast.7), custom_call_target="tpu_custom_call" | custom-call | flops 1000000 | bytes 4000000 | tf_op jit(solution)/shard_map/plan_cells/pallas_call | solution.py:252
  13.3 27.1 %all-to-all-done = bf16[32,8,2560]{2,1,0:T(8,128)(2,1)S(1)} async-done(((bf16[32,8,2560]{2,1,0:T(8,128)(2,1)}), bf16[32,8,2560]{2,1,0:T(8,128)(2,1)S(1)}, u32[]{:S(2)}, u32[]{:S(2)}) %all-to-all-start) | async-done | bytes 1310752 | tf_op jit(solution)/shard_map/all_to_all | solution.py:461
  40.4 0.0 copy-done
  40.4 3.2 %fit_steps.1 = (f32[32,128,128]{2,1,0:T(8,128)}, bf16[256,128]{1,0:T(8,128)(2,1)}) custom-call(s32[1,128]{1,0:T(1,128)S(1)} %get-tuple-element.7.refs_0_, bf16[256,2560]{1,0:T(8,128)(2,1)S(1)} %bitcast.5, f32[32,128,128]{2,1,0:T(8,128)S(1)} %get-tuple-element.8.refs_2_, bf16[2,256,128]{2,1,0:T(8,128)(2,1)S(1)} %copy-done, ...), custom_call_target="tpu_custom_call", output_to_operand_aliasing={{0}: (4, {})} | custom-call | tf_op jit(solution)/shard_map/fit_steps/pallas_call | solution.py:398
Async XLA Ops:
  3.1 37.3 %copy-start = (bf16[2,256,128]{2,1,0:T(8,128)(2,1)S(1)}, bf16[2,256,128]{2,1,0:T(8,128)(2,1)}, u32[]{:S(2)}) copy-start(bf16[2,256,128]{2,1,0:T(8,128)(2,1)} %refs_3_.1) | copy-start | bytes 393220
  3.2 37.3 %all-to-all-start = ((bf16[32,8,2560]{2,1,0:T(8,128)(2,1)}), bf16[32,8,2560]{2,1,0:T(8,128)(2,1)S(1)}, u32[]{:S(2)}, u32[]{:S(2)}) async-start(bf16[32,8,2560]{2,1,0:T(8,128)(2,1)} %pack_windows.1), calls=%async_computation | async-start | bytes 2621440 | tf_op jit(solution)/shard_map/all_to_all | solution.py:461
